TPU v7x, 128 devices: a whole 4x4x4 slice. The times are simulated.
128 devices in a mesh: rows: 32 (over y, x, z_lo), band: 4 (over z_hi, core).
Axes of the slice: x: 4, y: 4, z: 4 (z_hi: 2, z_lo: 2; z = z_hi * 2 + z_lo), core: 2. Of those that a mesh axis runs over, the one named last changes fastest.
Arguments:
- features: bfloat16 [8192, 128], P(('rows', 'band')), may hold values from -6 to 6
- deleted: int32 [8192], P(('rows', 'band')), may hold values 0 or 1
- proj_weight: bfloat16 [128, 64], replicated, may hold values from -0.5 to 0.5
- distance_embed: float32 [32, 128], P(None, 'band'), may hold values from -3 to 3
- conv_weight: float32 [8, 9, 32, 32], replicated, may hold values from -0.375 to 0.375
- conv_bias: float32 [8, 32], replicated, may hold values from -1.5 to 1.5
- dilations: int32 [4], replicated, may hold values from 1 to 8, as said below
Outputs:
- trunk_map: float32 [32, 128, 8192], P(None, 'band', 'rows')
Inputs may be any that keep to these rules, and one draw needn't show every extreme that they name: `dilations`: 8 occurs in every draw.
All inputs are finite; a program needn't handle non-finite values. No bound on the sum of `deleted` on one device may be relied on, other than what follows from the above.
Results may differ from a plain program's by a relative error of at most 0.00065.
Values may be sent and summed in bfloat16 or wider, within the bound.
A program may use at most 64 MiB of HBM per device.

v0:
```python
import functools

import jax
import jax.numpy as jnp
from jax import lax
from jax.experimental import pallas as pl
from jax.experimental.pallas import tpu as pltpu
from jax.sharding import PartitionSpec as P

PC = 32
DIAGS = 128
HALF = 64
BAND = 32
BINW = 256
MAXDIL = 8
BINS = 8192
W1 = 512
W2 = 384
FW = 640
R = 96
PAD = 8


def split_store(y_ref, j, x):
    hi = x.astype(jnp.bfloat16)
    lo = (x - hi.astype(jnp.float32)).astype(jnp.bfloat16)
    y_ref[j, 0:PC, :] = hi
    y_ref[j, PC:2 * PC, :] = lo


def taps(y_ref, j, k, weights):
    rows = jnp.concatenate([y_ref[j - k], y_ref[j], y_ref[j + k]], axis=0)
    return jnp.dot(weights, rows, preferred_element_type=jnp.float32)


def gather_taps(p, k, bias):
    width = p.shape[1]
    parts = [p[64 * b:64 * b + 32] + p[64 * b + 32:64 * b + 64] for b in range(3)]
    return (
        parts[1]
        + pltpu.roll(parts[0], k, 1)
        + pltpu.roll(parts[2], width - k, 1)
        + bias
    )


def valid_of(u, bins):
    low = jnp.maximum(0, HALF - u)
    high = jnp.where((u >= 0) & (u < DIAGS), jnp.minimum(BINS, BINS + HALF - u), 0)
    return (bins >= low) & (bins < high)


def blocks(dil_ref, first_block, w_ref, bias_ref, v_ref, ya, yb, first_u, bin0, width, rows_of, unroll):
    bins = lax.broadcasted_iota(jnp.int32, (1, width), 1) + bin0
    for n in range(4):
        k = dil_ref[first_block + n // 2]
        weights = w_ref[n]
        bias = jnp.broadcast_to(bias_ref[n], (PC, width))
        src, dst = (ya, yb) if n % 2 == 0 else (yb, ya)
        start, count = rows_of(n)

        def step(t, carry, n=n, k=k, weights=weights, bias=bias, src=src, dst=dst, start=start):
            base = start + t * unroll
            for s in range(unroll):
                j = base + s
                valid = valid_of(first_u + j, bins)
                branch = gather_taps(taps(src, j + PAD, k, weights), k, bias)
                branch = jnp.where(valid, branch, 0.0)
                if n % 2 == 1:
                    branch = v_ref[j] + branch
                    v_ref[j] = branch
                if n < 3:
                    split_store(dst, j + PAD, jnp.maximum(branch, 0.0))
            return carry

        lax.fori_loop(0, count // unroll, step, 0)


def first_half(dil_ref, meta_ref, feat_ref, proj_ref, emb_ref, w_ref, bias_ref, out_ref, v_ref, ya, yb, row_s, col_s, sem):
    half = meta_ref[0]
    bin0 = meta_ref[1] - 128
    first_u = half * 32
    projected = lax.dot_general(
        proj_ref[...], feat_ref[...], (((1,), (1,)), ((), ())), preferred_element_type=jnp.float32
    )
    row_s[...] = projected[:PC, 64:64 + W1]
    col_s[...] = projected[PC:]
    zero = jnp.zeros((PAD, 2 * PC, W1), jnp.bfloat16)
    for y in (ya, yb):
        y[0:PAD] = zero
        y[PAD + R:] = zero
    bins = lax.broadcasted_iota(jnp.int32, (1, W1), 1) + bin0
    lanes = lax.broadcasted_iota(jnp.int32, (PC, DIAGS), 1)

    def init(j, carry):
        u = first_u + j
        col = pltpu.roll(col_s[...], FW - u, 1)[:, :W1]
        emb = jnp.sum(jnp.where(lanes == u, emb_ref[...], 0.0), axis=1, keepdims=True)
        x = jnp.maximum(row_s[...] + col + emb, 0.0)
        x = jnp.where(valid_of(u, bins), x, 0.0)
        v_ref[j] = x
        split_store(ya, j + PAD, x)
        return carry

    lax.fori_loop(0, R, init, 0)

    def rows_of(n):
        return half * (8 * n + 8), 88 - 8 * n

    blocks(dil_ref, 0, w_ref, bias_ref, v_ref, ya, yb, first_u, bin0, W1, rows_of, 2)
    copy = pltpu.make_async_copy(v_ref.at[pl.ds(half * 32, 64)], out_ref, sem)
    copy.start()
    copy.wait()


def second_half(dil_ref, meta_ref, own_ref, other_ref, w_ref, bias_ref, out_ref, m_ref, v_ref, ya, yb, o_ref, sem, osem):
    half = meta_ref[0]
    bin0 = meta_ref[1] - 64
    first_u = meta_ref[2] * BAND - 32
    c1 = pltpu.make_async_copy(own_ref, m_ref.at[pl.ds(half * 64, 64)], sem.at[0])
    c2 = pltpu.make_async_copy(other_ref, m_ref.at[pl.ds(64 - half * 64, 64)], sem.at[1])
    c1.start()
    c2.start()
    zero = jnp.zeros((PAD, 2 * PC, W2), jnp.bfloat16)
    for y in (ya, yb):
        y[0:PAD] = zero
        y[PAD + R:] = zero
    c1.wait()
    c2.wait()
    bins = lax.broadcasted_iota(jnp.int32, (1, W2), 1) + bin0

    def init(j, carry):
        u = first_u + j
        ui = jnp.clip(u, 0, DIAGS - 1)
        own = pltpu.roll(m_ref[ui], W1 - 64, 1)[:, :W2]
        pi = jnp.clip(DIAGS - u, 0, DIAGS - 1)
        partner = pltpu.roll(m_ref[pi], (W1 - ui) % W1, 1)[:, :W2]
        partner = jnp.where(u > 0, partner, 0.0)
        x = jnp.where(valid_of(u, bins), 0.5 * (own + partner), 0.0)
        v_ref[j] = x
        split_store(ya, j + PAD, jnp.maximum(x, 0.0))
        return carry

    lax.fori_loop(0, R, init, 0)

    def rows_of(n):
        return 8 * n + 8, 80 - 16 * n

    blocks(dil_ref, 2, w_ref, bias_ref, v_ref, ya, yb, first_u, bin0, W2, rows_of, 2)
    for j in range(BAND):
        o_ref[j] = pltpu.roll(v_ref[32 + j], W2 - 64, 1)[:, :BINW]
        pltpu.make_async_copy(o_ref.at[j], out_ref.at[:, j, :], osem.at[j]).start()
    for j in range(BAND):
        pltpu.make_async_copy(o_ref.at[j], out_ref.at[:, j, :], osem.at[j]).wait()


smem = pl.BlockSpec(memory_space=pltpu.SMEM)
vmem = pl.BlockSpec(memory_space=pltpu.VMEM)
hbm = pl.BlockSpec(memory_space=pl.ANY)
LIMIT = 56 * 2 ** 20


def run_first(dil, meta, feat, proj, emb, w, bias):
    return pl.pallas_call(
        first_half,
        out_shape=jax.ShapeDtypeStruct((64, PC, W1), jnp.float32),
        in_specs=[smem, smem, vmem, vmem, vmem, vmem, vmem],
        out_specs=hbm,
        scratch_shapes=[
            pltpu.VMEM((R, PC, W1), jnp.float32),
            pltpu.VMEM((R + 2 * PAD, 2 * PC, W1), jnp.bfloat16),
            pltpu.VMEM((R + 2 * PAD, 2 * PC, W1), jnp.bfloat16),
            pltpu.VMEM((PC, W1), jnp.float32),
            pltpu.VMEM((PC, FW), jnp.float32),
            pltpu.SemaphoreType.DMA,
        ],
        compiler_params=pltpu.CompilerParams(vmem_limit_bytes=LIMIT),
        name="first_half",
    )(dil, meta, feat, proj, emb, w, bias)


def run_second(dil, meta, own, other, w, bias):
    return pl.pallas_call(
        second_half,
        out_shape=jax.ShapeDtypeStruct((PC, BAND, BINW), jnp.float32),
        in_specs=[smem, smem, hbm, hbm, vmem, vmem],
        out_specs=hbm,
        scratch_shapes=[
            pltpu.VMEM((DIAGS, PC, W1), jnp.float32),
            pltpu.VMEM((R, PC, W2), jnp.float32),
            pltpu.VMEM((R + 2 * PAD, 2 * PC, W2), jnp.bfloat16),
            pltpu.VMEM((R + 2 * PAD, 2 * PC, W2), jnp.bfloat16),
            pltpu.VMEM((BAND, PC, BINW), jnp.float32),
            pltpu.SemaphoreType.DMA((2,)),
            pltpu.SemaphoreType.DMA((BAND,)),
        ],
        compiler_params=pltpu.CompilerParams(vmem_limit_bytes=LIMIT),
        name="second_half",
    )(dil, meta, own, other, w, bias)


def prepare_weights(conv_weight):
    w = conv_weight.reshape(8, 3, 3, PC, PC).transpose(0, 2, 3, 1, 4)
    high = lax.reduce_precision(w, 8, 7)
    low = w - high
    both = jnp.stack([high, low], axis=2).astype(jnp.bfloat16)
    both = jnp.broadcast_to(both[:, :, :, :, :, None, :], (8, 3, 2, PC, 3, 2, PC))
    return both.reshape(8, 192, 192)


def body(features, deleted, proj_weight, distance_embed, conv_weight, conv_bias, dilations):
    band = lax.axis_index("band")
    row = lax.axis_index("rows")
    count = lax.axis_size("rows")
    kept = (1 - deleted).astype(jnp.bfloat16)
    masked = features * kept[:, None]
    own = lax.all_gather(masked, "band", axis=0, tiled=True)
    up = [(i, i + 1) for i in range(count - 1)]
    down = [(i + 1, i) for i in range(count - 1)]
    before = lax.ppermute(own[BINW - 192:], "rows", up)
    after = lax.ppermute(own[:192], "rows", down)
    feat = jnp.concatenate([before, own, after], axis=0)
    emb = lax.all_gather(distance_embed, "band", axis=1, tiled=True)
    w = prepare_weights(conv_weight)
    bias = conv_bias[:, :, None]
    meta = jnp.stack([band % 2, row * BINW, band]).astype(jnp.int32)
    mine = run_first(dilations, meta, feat, proj_weight.T, emb, w[:4], bias[:4])
    other = lax.ppermute(mine, "band", [(0, 1), (1, 0), (2, 3), (3, 2)])
    return run_second(dilations, meta, mine, other, w[4:], bias[4:])


def solution(mesh):
    return jax.shard_map(
        body,
        mesh=mesh,
        in_specs=(
            P(("rows", "band"), None),
            P(("rows", "band")),
            P(),
            P(None, "band"),
            P(),
            P(),
            P(),
        ),
        out_specs=P(None, "band", "rows"),
        check_vma=False,
    )
```

profile of v0, /device:TPU:17, one launch (start us, length us, event | category | flops | bytes accessed | tf_op | source)
XLA Modules:
  0.0 169.9 jit_solution(18009299208178774602)
XLA Ops:
  0.0 0.7 subtract_convert_fusion
  0.7 0.8 broadcast_multiply_fusion
  1.4 7.6 %all_gather.6 = bf16[256,128]{1,0:T(8,128)(2,1)S(1)} all-gather(bf16[64,128]{1,0:T(8,128)(2,1)S(1)} %broadcast_multiply_fusion), channel_id=1, replica_groups=mesh['rows'=32,'band'=4] {'band'}, dimensions={0}, use_global_device_ids=true | all-gather | bytes 81920 | tf_op jit(solution)/shard_map/all_gather | solution.py:217
  9.1 3.2 %collective-permute-start = (bf16[192,128]{1,0:T(8,128)(2,1)S(1)}, bf16[192,128]{1,0:T(8,128)(2,1)S(1)}, u32[]{:S(2)}, u32[]{:S(2)}) collective-permute-start(bf16[192,128]{1,0:T(8,128)(2,1)S(1)} %get-tuple-element.9), channel_id=1, source_target_pairs={{0,4},{4,8},{8,12},{12,16},{16,20},{20,24},{24,28},{28,32},{32,36}... | collective-permute-start | bytes 147464 | tf_op jit(solution)/shard_map/ppermute | solution.py:220
  12.3 5.1 %collective-permute-start.1 = (bf16[192,128]{1,0:T(8,128)(2,1)S(1)}, bf16[192,128]{1,0:T(8,128)(2,1)S(1)}, u32[]{:S(2)}, u32[]{:S(2)}) collective-permute-start(bf16[192,128]{1,0:T(8,128)(2,1)S(1)} %get-tuple-element.10), channel_id=1, source_target_pairs={{4,0},{8,4},{12,8},{16,12},{20,16},{24,20},{28,24},{32,28},{36,32}... | collective-permute-start | bytes 147464 | tf_op jit(solution)/shard_map/ppermute | solution.py:221
  17.4 0.8 slice_bitcast_fusion
  18.1 1.5 fusion.3
  19.6 0.0 copy-start
  19.6 0.2 fusion.5
  19.9 0.6 pad_add_fusion.meta_ref
  20.5 0.0 copy-done
  20.5 0.1 copy.12
  20.6 7.3 %all_gather.7 = f32[32,128]{0,1:T(8,128)S(1)} all-gather(f32[32,32]{0,1:T(8,128)S(1)} %copy.12), channel_id=1, replica_groups=mesh['rows'=32,'band'=4] {'band'}, dimensions={1}, use_global_device_ids=true | all-gather | bytes 20480 | tf_op jit(solution)/shard_map/all_gather | solution.py:223
  27.8 0.7 copy.14.emb_ref
  28.5 0.7 copy.15.bias_ref
  29.2 0.4 copy.13
  29.7 1.1 broadcast_in_dim.4
  30.7 1.6 slice.42.w_ref
  32.3 0.0 collective-permute-done
  32.4 0.0 collective-permute-done.1
  32.4 0.7 pad_maximum_fusion.1.feat_ref
  33.0 70.4 %first_half.1.own_ref = f32[64,32,512]{2,1,0:T(8,128)} custom-call(s32[4]{0:T(128)} %dil_ref.3, s32[3]{0:T(128)} %pad_add_fusion.meta_ref, bf16[640,128]{1,0:T(8,128)(2,1)} %pad_maximum_fusion.1.feat_ref, bf16[64,128]{1,0:T(8,128)(2,1)} %bitcast.20, f32[32,128]{1,0:T(8,128)} %copy.14.emb_ref, bf16[4,192,192]{2,1,0:T(8,128)(2,1)} %slice.42.w_ref, ...), custom_call_target="tpu_custom_call" | custom-call | tf_op jit(solution)/shard_map/first_half/pallas_call | solution.py:164
  103.4 0.3 collective-permute-start.2
  103.6 0.7 copy.17.bias_ref
  104.4 0.4 copy.16
  104.8 1.1 broadcast_in_dim.5
  105.8 1.7 slice.47.w_ref
  107.5 3.5 %collective-permute-done.2.other_ref = f32[64,32,512]{2,1,0:T(8,128)} collective-permute-done((f32[64,32,512]{2,1,0:T(8,128)}, f32[64,32,512]{2,1,0:T(8,128)}, u32[]{:S(2)}, u32[]{:S(2)}) %collective-permute-start.2) | collective-permute-done | bytes 4194336 | tf_op jit(solution)/shard_map/ppermute | solution.py:228
  111.0 58.9 %second_half.1 = f32[32,32,256]{2,1,0:T(8,128)} custom-call(s32[4]{0:T(128)} %dil_ref.3, s32[3]{0:T(128)} %pad_add_fusion.meta_ref, f32[64,32,512]{2,1,0:T(8,128)} %first_half.1.own_ref, f32[64,32,512]{2,1,0:T(8,128)} %collective-permute-done.2.other_ref, bf16[4,192,192]{2,1,0:T(8,128)(2,1)} %slice.47.w_ref, f32[4,32,1]{2,1,0:T(8,128)} %copy.17.bias_ref), custom_call_target="tpu_custom_call" | custom-call | tf_op jit(solution)/shard_map/second_half/pallas_call | solution.py:183
  (1 shorter events, 0.0 us)
Async XLA Ops:
  9.1 23.3 %collective-permute-start = (bf16[192,128]{1,0:T(8,128)(2,1)S(1)}, bf16[192,128]{1,0:T(8,128)(2,1)S(1)}, u32[]{:S(2)}, u32[]{:S(2)}) collective-permute-start(bf16[192,128]{1,0:T(8,128)(2,1)S(1)} %get-tuple-element.9), channel_id=1, source_target_pairs={{0,4},{4,8},{8,12},{12,16},{16,20},{20,24},{24,28},{28,32},{32,36}... | collective-permute-start | bytes 147464 | tf_op jit(solution)/shard_map/ppermute | solution.py:220
  12.3 20.1 %collective-permute-start.1 = (bf16[192,128]{1,0:T(8,128)(2,1)S(1)}, bf16[192,128]{1,0:T(8,128)(2,1)S(1)}, u32[]{:S(2)}, u32[]{:S(2)}) collective-permute-start(bf16[192,128]{1,0:T(8,128)(2,1)S(1)} %get-tuple-element.10), channel_id=1, source_target_pairs={{4,0},{8,4},{12,8},{16,12},{20,16},{24,20},{28,24},{32,28},{36,32}... | collective-permute-start | bytes 147464 | tf_op jit(solution)/shard_map/ppermute | solution.py:221
  19.6 0.9 copy-start
  103.4 7.6 %collective-permute-start.2 = (f32[64,32,512]{2,1,0:T(8,128)}, f32[64,32,512]{2,1,0:T(8,128)}, u32[]{:S(2)}, u32[]{:S(2)}) collective-permute-start(f32[64,32,512]{2,1,0:T(8,128)} %first_half.1.own_ref), channel_id=1, source_target_pairs={{0,1},{1,0},{2,3},{3,2},{4,5},{5,4},{6,7},{7,6},{8,9},{9,8},{10,11... | collective-permute-start | bytes 12582920 | tf_op jit(solution)/shard_map/ppermute | solution.py:228
where the time goes:
time: 170 us
  Pallas kernels  129 us (76%)
  blocking collectives  14.9 us (9%)
  local copies, waits for them, and re-layouts  9.18 us (5%)
  starting transfers between devices  8.55 us (5%)
  other arithmetic  4.43 us (3%)
  waiting for transfers between devices  3.47 us (2%)
    pallas_call x1, Pallas kernels, run_first(): pl.pallas_call(first_half, out_shape=jax.ShapeDtypeStruct((64, PC, W1), j...  70.4 us
    pallas_call x1, Pallas kernels, run_second(): pl.pallas_call(second_half, out_shape=jax.ShapeDtypeStruct((PC, BAND, BIN...  58.9 us
    all_gather x1, blocking collectives, body(): own = lax.all_gather(masked, 'band', axis=0, tiled=True)  7.59 us
    all_gather x1, blocking collectives, body(): emb = lax.all_gather(distance_embed, 'band', axis=1, tiled=True)  7.29 us
    ppermute x1, starting transfers between devices, body(): after = lax.ppermute(own[:192], 'rows', down)  5.09 us
    slice x4, local copies, waits for them, and re-layouts, body(): return run_second(dilations, meta, mine, other, w[4:], bias[4:])  3.55 us
    ppermute x1, waiting for transfers between devices, body(): other = lax.ppermute(mine, 'band', [(0, 1), (1, 0), (2, 3), (3, 2)])  3.47 us
  transfers between devices with their start and end apart: 3, of which 1 were waited for; matrix products, arithmetic and copies ran while one was open for 7% of the time, Pallas kernels for 0%

commit v1 on v0

--- a/solution.py
+++ b/solution.py
@@ -92,7 +92,12 @@
     bins = lax.broadcasted_iota(jnp.int32, (1, W1), 1) + bin0
     lanes = lax.broadcasted_iota(jnp.int32, (PC, DIAGS), 1)
 
-    def init(j, carry):
+    def init(t, carry):
+        for s in range(4):
+            start(t * 4 + s)
+        return carry
+
+    def start(j):
         u = first_u + j
         col = pltpu.roll(col_s[...], FW - u, 1)[:, :W1]
         emb = jnp.sum(jnp.where(lanes == u, emb_ref[...], 0.0), axis=1, keepdims=True)
@@ -100,14 +105,13 @@
         x = jnp.where(valid_of(u, bins), x, 0.0)
         v_ref[j] = x
         split_store(ya, j + PAD, x)
-        return carry
-
-    lax.fori_loop(0, R, init, 0)
+
+    lax.fori_loop(0, R // 4, init, 0)
 
     def rows_of(n):
         return half * (8 * n + 8), 88 - 8 * n
 
-    blocks(dil_ref, 0, w_ref, bias_ref, v_ref, ya, yb, first_u, bin0, W1, rows_of, 2)
+    blocks(dil_ref, 0, w_ref, bias_ref, v_ref, ya, yb, first_u, bin0, W1, rows_of, 8)
     copy = pltpu.make_async_copy(v_ref.at[pl.ds(half * 32, 64)], out_ref, sem)
     copy.start()
     copy.wait()
@@ -129,7 +133,12 @@
     c2.wait()
     bins = lax.broadcasted_iota(jnp.int32, (1, W2), 1) + bin0
 
-    def init(j, carry):
+    def init(t, carry):
+        for s in range(4):
+            start(t * 4 + s)
+        return carry
+
+    def start(j):
         u = first_u + j
         ui = jnp.clip(u, 0, DIAGS - 1)
         own = pltpu.roll(m_ref[ui], W1 - 64, 1)[:, :W2]
@@ -139,14 +148,13 @@
         x = jnp.where(valid_of(u, bins), 0.5 * (own + partner), 0.0)
         v_ref[j] = x
         split_store(ya, j + PAD, jnp.maximum(x, 0.0))
-        return carry
-
-    lax.fori_loop(0, R, init, 0)
+
+    lax.fori_loop(0, R // 4, init, 0)
 
     def rows_of(n):
         return 8 * n + 8, 80 - 16 * n
 
-    blocks(dil_ref, 2, w_ref, bias_ref, v_ref, ya, yb, first_u, bin0, W2, rows_of, 2)
+    blocks(dil_ref, 2, w_ref, bias_ref, v_ref, ya, yb, first_u, bin0, W2, rows_of, 8)
     for j in range(BAND):
         o_ref[j] = pltpu.roll(v_ref[32 + j], W2 - 64, 1)[:, :BINW]
         pltpu.make_async_copy(o_ref.at[j], out_ref.at[:, j, :], osem.at[j]).start()

time: 170 us -> 108 us (0.64)
  Pallas kernels: 129 us -> 67.4 us
    pallas_call x1, Pallas kernels: 70.4 us -> 35.5 us  [run_first(): pl.pallas_call(first_half, out_shape=jax.ShapeDtypeStruct((64, PC, W1), j...]
    pallas_call x1, Pallas kernels: 58.9 us -> 31.9 us  [run_second(): pl.pallas_call(second_half, out_shape=jax.ShapeDtypeStruct((PC, BAND, BIN...]
  transfers between devices with their start and end apart: 3 -> 3, of which waited for: 1 -> 1; matrix products, arithmetic and copies ran while one was open for 7% -> 11% of each run, Pallas kernels for 0% -> 0%
where the time goes in v1:
time: 108 us
  Pallas kernels  67.4 us (62%)
  blocking collectives  14.9 us (14%)
  local copies, waits for them, and re-layouts  9.18 us (8%)
  starting transfers between devices  8.54 us (8%)
  other arithmetic  4.43 us (4%)
  waiting for transfers between devices  3.48 us (3%)
    pallas_call x1, Pallas kernels, run_first(): pl.pallas_call(first_half, out_shape=jax.ShapeDtypeStruct((64, PC, W1), j...  35.5 us
    pallas_call x1, Pallas kernels, run_second(): pl.pallas_call(second_half, out_shape=jax.ShapeDtypeStruct((PC, BAND, BIN...  31.9 us
    all_gather x1, blocking collectives, body(): own = lax.all_gather(masked, 'band', axis=0, tiled=True)  7.59 us
    all_gather x1, blocking collectives, body(): emb = lax.all_gather(distance_embed, 'band', axis=1, tiled=True)  7.29 us
    ppermute x1, starting transfers between devices, body(): after = lax.ppermute(own[:192], 'rows', down)  5.09 us
    slice x4, local copies, waits for them, and re-layouts, body(): return run_second(dilations, meta, mine, other, w[4:], bias[4:])  3.55 us
    ppermute x1, waiting for transfers between devices, body(): other = lax.ppermute(mine, 'band', [(0, 1), (1, 0), (2, 3), (3, 2)])  3.48 us
    ppermute x1, starting transfers between devices, body(): before = lax.ppermute(own[BINW - 192:], 'rows', up)  3.2 us
  transfers between devices with their start and end apart: 3, of which 1 were waited for; matrix products, arithmetic and copies ran while one was open for 11% of the time, Pallas kernels for 0%

profile of v1, /device:TPU:17, one launch (start us, length us, event | category | flops | bytes accessed | tf_op | source)
XLA Modules:
  0.0 108.0 jit_solution(1409224367058660668)
XLA Ops:
  0.0 0.7 subtract_convert_fusion
  0.7 0.8 broadcast_multiply_fusion
  1.4 7.6 %all_gather.6 = bf16[256,128]{1,0:T(8,128)(2,1)S(1)} all-gather(bf16[64,128]{1,0:T(8,128)(2,1)S(1)} %broadcast_multiply_fusion), channel_id=1, replica_groups=mesh['rows'=32,'band'=4] {'band'}, dimensions={0}, use_global_device_ids=true | all-gather | bytes 81920 | tf_op jit(solution)/shard_map/all_gather | solution.py:225
  9.1 3.2 %collective-permute-start = (bf16[192,128]{1,0:T(8,128)(2,1)S(1)}, bf16[192,128]{1,0:T(8,128)(2,1)S(1)}, u32[]{:S(2)}, u32[]{:S(2)}) collective-permute-start(bf16[192,128]{1,0:T(8,128)(2,1)S(1)} %get-tuple-element.9), channel_id=1, source_target_pairs={{0,4},{4,8},{8,12},{12,16},{16,20},{20,24},{24,28},{28,32},{32,36}... | collective-permute-start | bytes 147464 | tf_op jit(solution)/shard_map/ppermute | solution.py:228
  12.3 5.1 %collective-permute-start.1 = (bf16[192,128]{1,0:T(8,128)(2,1)S(1)}, bf16[192,128]{1,0:T(8,128)(2,1)S(1)}, u32[]{:S(2)}, u32[]{:S(2)}) collective-permute-start(bf16[192,128]{1,0:T(8,128)(2,1)S(1)} %get-tuple-element.10), channel_id=1, source_target_pairs={{4,0},{8,4},{12,8},{16,12},{20,16},{24,20},{28,24},{32,28},{36,32}... | collective-permute-start | bytes 147464 | tf_op jit(solution)/shard_map/ppermute | solution.py:229
  17.4 0.8 slice_bitcast_fusion
  18.1 1.5 %fusion.3 = (bf16[8,3,1,32,3,1,32]{6,3,1,4,0,5,2:T(8,128)(2,1)S(1)}, bf16[8,3,1,32,3,1,32]{6,3,1,4,0,5,2:T(8,128)(2,1)S(1)}) fusion(f32[8,3,32,3,32]{4,2,1,3,0:T(8,128)} %bitcast.19), kind=kLoop, calls=%fused_computation.7 | loop fusion | flops 294912 | bytes 589824 | tf_op jit(solution)/shard_map/stack | solution.py:214
  19.6 0.0 copy-start
  19.6 0.2 fusion.5
  19.9 0.6 pad_add_fusion.meta_ref
  20.5 0.0 copy-done
  20.5 0.1 copy.12
  20.6 7.3 %all_gather.7 = f32[32,128]{0,1:T(8,128)S(1)} all-gather(f32[32,32]{0,1:T(8,128)S(1)} %copy.12), channel_id=1, replica_groups=mesh['rows'=32,'band'=4] {'band'}, dimensions={1}, use_global_device_ids=true | all-gather | bytes 20480 | tf_op jit(solution)/shard_map/all_gather | solution.py:231
  27.8 0.7 copy.14.emb_ref
  28.5 0.7 copy.15.bias_ref
  29.2 0.4 copy.13
  29.7 1.1 broadcast_in_dim.4
  30.7 1.6 %slice.42.w_ref = bf16[4,192,192]{2,1,0:T(8,128)(2,1)} reshape(bf16[4,3,2,32,3,2,32]{6,5,4,3,2,1,0:T(2,128)(2,1)S(1)} %broadcast_in_dim.4) | data formatting | bytes 589824 | tf_op jit(solution)/shard_map/slice | solution.py:235
  32.3 0.0 collective-permute-done
  32.4 0.0 collective-permute-done.1
  32.4 0.7 pad_maximum_fusion.1.feat_ref
  33.0 35.5 %first_half.1.own_ref = f32[64,32,512]{2,1,0:T(8,128)} custom-call(s32[4]{0:T(128)} %dil_ref.3, s32[3]{0:T(128)} %pad_add_fusion.meta_ref, bf16[640,128]{1,0:T(8,128)(2,1)} %pad_maximum_fusion.1.feat_ref, bf16[64,128]{1,0:T(8,128)(2,1)} %bitcast.20, f32[32,128]{1,0:T(8,128)} %copy.14.emb_ref, bf16[4,192,192]{2,1,0:T(8,128)(2,1)} %slice.42.w_ref, ...), custom_call_target="tpu_custom_call" | custom-call | tf_op jit(solution)/shard_map/first_half/pallas_call | solution.py:172
  68.5 0.2 collective-permute-start.2
  68.8 0.7 copy.17.bias_ref
  69.5 0.4 copy.16
  69.9 1.1 broadcast_in_dim.5
  71.0 1.7 %slice.47.w_ref = bf16[4,192,192]{2,1,0:T(8,128)(2,1)} reshape(bf16[4,3,2,32,3,2,32]{6,5,4,3,2,1,0:T(2,128)(2,1)S(1)} %broadcast_in_dim.5) | data formatting | bytes 589824 | tf_op jit(solution)/shard_map/slice | solution.py:237
  72.6 3.5 %collective-permute-done.2.other_ref = f32[64,32,512]{2,1,0:T(8,128)} collective-permute-done((f32[64,32,512]{2,1,0:T(8,128)}, f32[64,32,512]{2,1,0:T(8,128)}, u32[]{:S(2)}, u32[]{:S(2)}) %collective-permute-start.2) | collective-permute-done | bytes 4194336 | tf_op jit(solution)/shard_map/ppermute | solution.py:236
  76.1 31.9 %second_half.1 = f32[32,32,256]{2,1,0:T(8,128)} custom-call(s32[4]{0:T(128)} %dil_ref.3, s32[3]{0:T(128)} %pad_add_fusion.meta_ref, f32[64,32,512]{2,1,0:T(8,128)} %first_half.1.own_ref, f32[64,32,512]{2,1,0:T(8,128)} %collective-permute-done.2.other_ref, bf16[4,192,192]{2,1,0:T(8,128)(2,1)} %slice.47.w_ref, f32[4,32,1]{2,1,0:T(8,128)} %copy.17.bias_ref), custom_call_target="tpu_custom_call" | custom-call | tf_op jit(solution)/shard_map/second_half/pallas_call | solution.py:191
  (1 shorter events, 0.0 us)
Async XLA Ops:
  9.1 23.3 %collective-permute-start = (bf16[192,128]{1,0:T(8,128)(2,1)S(1)}, bf16[192,128]{1,0:T(8,128)(2,1)S(1)}, u32[]{:S(2)}, u32[]{:S(2)}) collective-permute-start(bf16[192,128]{1,0:T(8,128)(2,1)S(1)} %get-tuple-element.9), channel_id=1, source_target_pairs={{0,4},{4,8},{8,12},{12,16},{16,20},{20,24},{24,28},{28,32},{32,36}... | collective-permute-start | bytes 147464 | tf_op jit(solution)/shard_map/ppermute | solution.py:228
  12.3 20.1 %collective-permute-start.1 = (bf16[192,128]{1,0:T(8,128)(2,1)S(1)}, bf16[192,128]{1,0:T(8,128)(2,1)S(1)}, u32[]{:S(2)}, u32[]{:S(2)}) collective-permute-start(bf16[192,128]{1,0:T(8,128)(2,1)S(1)} %get-tuple-element.10), channel_id=1, source_target_pairs={{4,0},{8,4},{12,8},{16,12},{20,16},{24,20},{28,24},{32,28},{36,32}... | collective-permute-start | bytes 147464 | tf_op jit(solution)/shard_map/ppermute | solution.py:229
  19.6 0.9 copy-start
  68.5 7.6 %collective-permute-start.2 = (f32[64,32,512]{2,1,0:T(8,128)}, f32[64,32,512]{2,1,0:T(8,128)}, u32[]{:S(2)}, u32[]{:S(2)}) collective-permute-start(f32[64,32,512]{2,1,0:T(8,128)} %first_half.1.own_ref), channel_id=1, source_target_pairs={{0,1},{1,0},{2,3},{3,2},{4,5},{5,4},{6,7},{7,6},{8,9},{9,8},{10,11... | collective-permute-start | bytes 12582920 | tf_op jit(solution)/shard_map/ppermute | solution.py:236

commit v2 on v1

v2 whole, which is shorter than its diff:
```python
import functools

import jax
import jax.numpy as jnp
from jax import lax
from jax.experimental import pallas as pl
from jax.experimental.pallas import tpu as pltpu
from jax.sharding import PartitionSpec as P

PC = 32
DIAGS = 128
HALF = 64
BAND = 32
BINW = 256
MAXDIL = 8
BINS = 8192
W1 = 512
W2 = 384
FW = 640
R = 96
PAD = 8
UNROLL = 16
ROWS = 32
MESH = pl.DeviceIdType.MESH


def split_store(y_ref, j, x):
    hi = x.astype(jnp.bfloat16)
    lo = (x - hi.astype(jnp.float32)).astype(jnp.bfloat16)
    y_ref[j, 0:PC, :] = hi
    y_ref[j, PC:2 * PC, :] = lo


def gather_taps(p, k, bias):
    width = p.shape[1]
    parts = [p[64 * b:64 * b + 32] + p[64 * b + 32:64 * b + 64] for b in range(3)]
    return (
        parts[1]
        + pltpu.roll(parts[0], k, 1)
        + pltpu.roll(parts[2], width - k, 1)
        + bias
    )


def valid_of(u, bins):
    low = jnp.maximum(0, HALF - u)
    high = jnp.where((u >= 0) & (u < DIAGS), jnp.minimum(BINS, BINS + HALF - u), 0)
    return (bins >= low) & (bins < high)


def conv(k, weights, bias, src, dst, v_ref, first_u, bins, start, count, residual, done=None):
    width = bins.shape[1]
    cat = 2 if width % 256 else 1

    def group(base, rows):
        for g in range(0, rows, cat):
            stack = [
                jnp.concatenate([src[j - k], src[j], src[j + k]], axis=0)
                for j in [base + g + c + PAD for c in range(cat)]
            ]
            stack = stack[0] if cat == 1 else jnp.concatenate(stack, axis=1)
            p = jnp.dot(weights, stack, preferred_element_type=jnp.float32)
            for c in range(cat):
                j = base + g + c
                branch = gather_taps(p[:, c * width:(c + 1) * width], k, bias)
                branch = jnp.where(valid_of(first_u + j, bins), branch, 0.0)
                if residual:
                    branch = v_ref[j] + branch
                    v_ref[j] = branch
                if dst is not None:
                    split_store(dst, j + PAD, jnp.maximum(branch, 0.0))
        if done is not None:
            done(base, rows)

    def step(t, carry):
        group(start + t * UNROLL, UNROLL)
        return carry

    lax.fori_loop(0, count // UNROLL, step, 0)
    if count % UNROLL:
        group(start + count // UNROLL * UNROLL, count % UNROLL)


def blocks(dil_ref, first_block, w_ref, bias_ref, v_ref, ya, yb, first_u, bins, rows_of, done=None):
    for n in range(4):
        src, dst = (ya, yb) if n % 2 == 0 else (yb, ya)
        start, count = rows_of(n)
        bias = jnp.concatenate([bias_ref[n]] * (bins.shape[1] // 128), axis=1)
        conv(
            dil_ref[first_block + n // 2], w_ref[n], bias, src, dst if n < 3 else None, v_ref,
            first_u, bins, start, count, n % 2 == 1, done if n == 3 else None,
        )


def gather(feat_ref, del_ref, emb_ref, cw_ref, cb_ref, feat_out, emb_out, w_first, w_second, bias_first, bias_second,
           kept, land, emb_land, send, recv, esend, erecv):
    row = lax.axis_index("rows")
    band = lax.axis_index("band")
    near = [(row, lax.rem(band + d, 4)) for d in range(1, 4)]
    after = [(lax.rem(row + 1, ROWS), d) for d in range(4)]
    before = [(lax.rem(row + ROWS - 1, ROWS), d) for d in range(4)]
    barrier = pltpu.get_barrier_semaphore()
    for r, b in near + after + before:
        pl.semaphore_signal(barrier, inc=1, device_id={"rows": r, "band": b}, device_id_type=MESH)

    same = lax.broadcasted_iota(jnp.int32, (64, 64), 0) == lax.broadcasted_iota(jnp.int32, (64, 64), 1)
    gone = jnp.sum(jnp.where(same, del_ref[...].astype(jnp.float32), 0.0), axis=1, keepdims=True)
    kept[...] = (feat_ref[...].astype(jnp.float32) * (1.0 - gone)).astype(jnp.bfloat16)

    pl.semaphore_wait(barrier, 11)
    copies = []

    def send_to(r, b, slot, index):
        copies.append(pltpu.make_async_remote_copy(
            kept, land.at[slot, band], send.at[index], recv.at[slot, band],
            device_id={"rows": r, "band": b}, device_id_type=MESH))

    for d, (r, b) in enumerate(near):
        send_to(r, b, 1, d)
    for d, (r, b) in enumerate(after):
        send_to(r, b, 0, 3 + d)
    for d, (r, b) in enumerate(before):
        send_to(r, b, 2, 7 + d)
    for d, (r, b) in enumerate(near):
        copies.append(pltpu.make_async_remote_copy(
            emb_ref, emb_land.at[band], esend.at[d], erecv.at[band],
            device_id={"rows": r, "band": b}, device_id_type=MESH))
    for copy in copies:
        copy.start()
    land[1, band] = kept[...]
    emb_land[band] = emb_ref[...]

    square = lax.broadcasted_iota(jnp.int32, (PC, PC), 0) == lax.broadcasted_iota(jnp.int32, (PC, PC), 1)

    def weights(first, w_out, bias_out, n, carry):
        for b in range(3):
            t = [cw_ref[first + n, 3 * a + b] for a in range(3)]
            wide = jnp.concatenate([t[0], t[0], t[1], t[1], t[2], t[2]], axis=1)
            high = wide.astype(jnp.bfloat16)
            w_out[n, 64 * b:64 * b + 32, :] = high
            w_out[n, 64 * b + 32:64 * b + 64, :] = (wide - high.astype(jnp.float32)).astype(jnp.bfloat16)
        column = jnp.sum(jnp.where(square, cb_ref[first + n], 0.0), axis=1, keepdims=True)
        bias_out[n] = jnp.broadcast_to(column, (PC, 128))
        return carry

    lax.fori_loop(0, 4, functools.partial(weights, 0, w_first, bias_first), 0)
    lax.fori_loop(0, 4, functools.partial(weights, 4, w_second, bias_second), 0)

    def arrived(buf, sem):
        pltpu.make_async_copy(buf, buf, sem).wait()

    for d in range(1, 4):
        b = lax.rem(band + d, 4)
        arrived(land.at[1, b], recv.at[1, b])
        arrived(emb_land.at[b], erecv.at[b])
    for d in range(4):
        arrived(land.at[0, d], recv.at[0, d])
        arrived(land.at[2, d], recv.at[2, d])
    for i, (s, b) in enumerate([(0, 1), (0, 2), (0, 3), (1, 0), (1, 1), (1, 2), (1, 3), (2, 0), (2, 1), (2, 2)]):
        feat_out[64 * i:64 * i + 64] = land[s, b]
    emb_out[...] = emb_land[...]
    for copy in copies:
        copy.wait_send()


def first_half(dil_ref, feat_ref, proj_ref, emb_ref, w_ref, bias_ref, out_ref, v_ref, ya, yb, row_s, col_s, sem):
    half = lax.rem(lax.axis_index("band"), 2)
    bin0 = lax.axis_index("rows") * BINW - 128
    first_u = half * 32
    projected = lax.dot_general(
        proj_ref[...], feat_ref[...], (((0,), (1,)), ((), ())), preferred_element_type=jnp.float32
    )
    row_s[...] = projected[:PC, 64:64 + W1]
    col_s[...] = projected[PC:]
    zero = jnp.zeros((PAD, 2 * PC, W1), jnp.bfloat16)
    for y in (ya, yb):
        y[0:PAD] = zero
        y[PAD + R:] = zero
    bins = lax.broadcasted_iota(jnp.int32, (1, W1), 1) + bin0
    lanes = lax.broadcasted_iota(jnp.int32, (PC, BAND), 1)

    def init(t, carry):
        for s in range(4):
            start(t * 4 + s)
        return carry

    def start(j):
        u = first_u + j
        col = pltpu.roll(col_s[...], FW - u, 1)[:, :W1]
        emb = jnp.sum(jnp.where(lanes == lax.rem(u, BAND), emb_ref[lax.div(u, BAND)], 0.0), axis=1, keepdims=True)
        x = jnp.maximum(row_s[...] + col + emb, 0.0)
        x = jnp.where(valid_of(u, bins), x, 0.0)
        v_ref[j] = x
        split_store(ya, j + PAD, x)

    lax.fori_loop(0, R // 4, init, 0)

    def rows_of(n):
        return half * (8 * n + 8), 88 - 8 * n

    def out_copy(base, rows):
        return pltpu.make_async_copy(
            v_ref.at[pl.ds(base, rows)], out_ref.at[pl.ds(base - half * 32, rows)], sem)

    blocks(dil_ref, 0, w_ref, bias_ref, v_ref, ya, yb, first_u, bins, rows_of,
           lambda base, rows: out_copy(base, rows).start())
    out_copy(half * 32, 64).wait()


def second_half(dil_ref, own_ref, other_ref, w_ref, bias_ref, out_ref, m_ref, v_ref, ya, yb, o_ref, sem, osem):
    band = lax.axis_index("band")
    half = lax.rem(band, 2)
    bin0 = lax.axis_index("rows") * BINW - 64
    first_u = band * BAND - 32
    c1 = pltpu.make_async_copy(own_ref, m_ref.at[pl.ds(half * 64, 64)], sem.at[0])
    c2 = pltpu.make_async_copy(other_ref, m_ref.at[pl.ds(64 - half * 64, 64)], sem.at[1])
    c1.start()
    c2.start()
    zero = jnp.zeros((PAD, 2 * PC, W2), jnp.bfloat16)
    for y in (ya, yb):
        y[0:PAD] = zero
        y[PAD + R:] = zero
    c1.wait()
    c2.wait()
    bins = lax.broadcasted_iota(jnp.int32, (1, W2), 1) + bin0

    def init(t, carry):
        for s in range(4):
            start(t * 4 + s)
        return carry

    def start(j):
        u = first_u + j
        ui = jnp.clip(u, 0, DIAGS - 1)
        own = pltpu.roll(m_ref[ui], W1 - 64, 1)[:, :W2]
        pi = jnp.clip(DIAGS - u, 0, DIAGS - 1)
        partner = pltpu.roll(m_ref[pi], (W1 - ui) % W1, 1)[:, :W2]
        partner = jnp.where(u > 0, partner, 0.0)
        x = jnp.where(valid_of(u, bins), 0.5 * (own + partner), 0.0)
        v_ref[j] = x
        split_store(ya, j + PAD, jnp.maximum(x, 0.0))

    lax.fori_loop(0, R // 4, init, 0)

    def rows_of(n):
        return 8 * n + 8, 80 - 16 * n

    def out_copy(j):
        return pltpu.make_async_copy(o_ref.at[j], out_ref.at[:, j, :], osem.at[j])

    def done(base, rows):
        for r in range(rows):
            j = base - 32 + r
            o_ref[j] = pltpu.roll(v_ref[j + 32], W2 - 64, 1)[:, :BINW]
            out_copy(j).start()

    blocks(dil_ref, 2, w_ref, bias_ref, v_ref, ya, yb, first_u, bins, rows_of, done)
    for j in range(BAND):
        out_copy(j).wait()


smem = pl.BlockSpec(memory_space=pltpu.SMEM)
vmem = pl.BlockSpec(memory_space=pltpu.VMEM)
hbm = pl.BlockSpec(memory_space=pl.ANY)
LIMIT = 56 * 2 ** 20


def run_gather(features, deleted, emb, conv_weight, conv_bias):
    return pl.pallas_call(
        gather,
        out_shape=[
            jax.ShapeDtypeStruct((FW, 128), jnp.bfloat16),
            jax.ShapeDtypeStruct((4, PC, BAND), jnp.float32),
            jax.ShapeDtypeStruct((4, 192, 192), jnp.bfloat16),
            jax.ShapeDtypeStruct((4, 192, 192), jnp.bfloat16),
            jax.ShapeDtypeStruct((4, PC, 128), jnp.float32),
            jax.ShapeDtypeStruct((4, PC, 128), jnp.float32),
        ],
        in_specs=[vmem] * 5,
        out_specs=[vmem] * 6,
        scratch_shapes=[
            pltpu.VMEM((64, 128), jnp.bfloat16),
            pltpu.VMEM((3, 4, 64, 128), jnp.bfloat16),
            pltpu.VMEM((4, PC, BAND), jnp.float32),
            pltpu.SemaphoreType.DMA((11,)),
            pltpu.SemaphoreType.DMA((3, 4)),
            pltpu.SemaphoreType.DMA((3,)),
            pltpu.SemaphoreType.DMA((4,)),
        ],
        compiler_params=pltpu.CompilerParams(collective_id=0, has_side_effects=True),
        name="gather",
    )(features, deleted.reshape(1, 64), emb, conv_weight, conv_bias.reshape(8, 1, PC))


def run_first(dil, feat, proj, emb, w, bias):
    return pl.pallas_call(
        first_half,
        out_shape=jax.ShapeDtypeStruct((64, PC, W1), jnp.float32),
        in_specs=[
            smem, vmem, vmem, vmem,
            vmem, vmem,
        ],
        out_specs=hbm,
        scratch_shapes=[
            pltpu.VMEM((R, PC, W1), jnp.float32),
            pltpu.VMEM((R + 2 * PAD, 2 * PC, W1), jnp.bfloat16),
            pltpu.VMEM((R + 2 * PAD, 2 * PC, W1), jnp.bfloat16),
            pltpu.VMEM((PC, W1), jnp.float32),
            pltpu.VMEM((PC, FW), jnp.float32),
            pltpu.SemaphoreType.DMA,
        ],
        compiler_params=pltpu.CompilerParams(vmem_limit_bytes=LIMIT),
        name="first_half",
    )(dil, feat, proj, emb, w, bias)


def run_second(dil, own, other, w, bias):
    return pl.pallas_call(
        second_half,
        out_shape=jax.ShapeDtypeStruct((PC, BAND, BINW), jnp.float32),
        in_specs=[
            smem, hbm, hbm,
            vmem, vmem,
        ],
        out_specs=hbm,
        scratch_shapes=[
            pltpu.VMEM((DIAGS, PC, W1), jnp.float32),
            pltpu.VMEM((R, PC, W2), jnp.float32),
            pltpu.VMEM((R + 2 * PAD, 2 * PC, W2), jnp.bfloat16),
            pltpu.VMEM((R + 2 * PAD, 2 * PC, W2), jnp.bfloat16),
            pltpu.VMEM((BAND, PC, BINW), jnp.float32),
            pltpu.SemaphoreType.DMA((2,)),
            pltpu.SemaphoreType.DMA((BAND,)),
        ],
        compiler_params=pltpu.CompilerParams(vmem_limit_bytes=LIMIT),
        name="second_half",
    )(dil, own, other, w, bias)


def body(features, deleted, proj_weight, distance_embed, conv_weight, conv_bias, dilations):
    feat, emb, w_first, w_second, bias_first, bias_second = run_gather(features, deleted, distance_embed, conv_weight, conv_bias)
    mine = run_first(dilations, feat, proj_weight, emb, w_first, bias_first)
    other = lax.ppermute(mine, "band", [(0, 1), (1, 0), (2, 3), (3, 2)])
    return run_second(dilations, mine, other, w_second, bias_second)


def solution(mesh):
    return jax.shard_map(
        body,
        mesh=mesh,
        in_specs=(
            P(("rows", "band"), None),
            P(("rows", "band")),
            P(),
            P(None, "band"),
            P(),
            P(),
            P(),
        ),
        out_specs=P(None, "band", "rows"),
        check_vma=False,
    )
```

time: 108 us -> 82.9 us (0.77)
  the two profiles are of different devices: /device:TPU:17 before, /device:TPU:1 now
where the time goes in v2:
time: 82.9 us; the launch traced here: 82.7 us
  Pallas kernels  71.8 us (87%)
  waiting for transfers between devices  7 us (8%)
  local copies, waits for them, and re-layouts  3.41 us (4%)
    pallas_call x1, Pallas kernels, run_first(): pl.pallas_call(first_half, out_shape=jax.ShapeDtypeStruct((64, PC, W1), j...  29.5 us
    pallas_call x1, Pallas kernels, run_second(): pl.pallas_call(second_half, out_shape=jax.ShapeDtypeStruct((PC, BAND, BIN...  25.3 us
    pallas_call x1, Pallas kernels, run_gather(): pl.pallas_call(gather, out_shape=[jax.ShapeDtypeStruct((FW, 128), jnp.bfl...  16.9 us
    ppermute x1, waiting for transfers between devices, body(): other = lax.ppermute(mine, 'band', [(0, 1), (1, 0), (2, 3), (3, 2)])  7 us
    unnamed x3, local copies, waits for them, and re-layouts  3.41 us
  transfers between devices with their start and end apart: 1, of which 1 were waited for; matrix products, arithmetic and copies ran while one was open for 0% of the time, Pallas kernels for 0%

profile of v2, /device:TPU:1, one launch (start us, length us, event | category | flops | bytes accessed | tf_op | source)
XLA Modules:
  0.0 82.7 jit_solution(7109616999655519129)
XLA Ops:
  0.0 1.4 %copy.8.proj_ref = bf16[128,64]{1,0:T(8,128)(2,1)} copy(bf16[128,64]{0,1:T(8,128)(2,1)} %param.9) | data formatting | bytes 32768 | tf_op args[2]
  1.4 16.9 %gather.1 = (bf16[640,128]{1,0:T(8,128)(2,1)}, f32[4,32,32]{2,1,0:T(8,128)}, bf16[4,192,192]{2,1,0:T(8,128)(2,1)}, bf16[4,192,192]{2,1,0:T(8,128)(2,1)}, f32[4,32,128]{2,1,0:T(8,128)}, /*index=5*/f32[4,32,128]{2,1,0:T(8,128)}) custom-call(bf16[64,128]{1,0:T(8,128)(2,1)} %feat_ref.1, s32[1,64]{1,0:T(1,128)} %bitcast.3, f32[32,32]{1,0:T(8,128)} %emb_ref.1, ...), custom_call_target="tpu_custom_call" | custom-call | tf_op jit(solution)/shard_map/gather/pallas_call | solution.py:269
  18.3 29.5 %first_half.1.own_ref = f32[64,32,512]{2,1,0:T(8,128)} custom-call(s32[4]{0:T(128)} %dil_ref.3, bf16[640,128]{1,0:T(8,128)(2,1)} %get-tuple-element.11.feat_ref, bf16[128,64]{1,0:T(8,128)(2,1)} %copy.8.proj_ref, f32[4,32,32]{2,1,0:T(8,128)} %get-tuple-element.12.emb_ref, bf16[4,192,192]{2,1,0:T(8,128)(2,1)} %get-tuple-element.13.w_ref, ...), custom_call_target="tpu_custom_call" | custom-call | tf_op jit(solution)/shard_map/first_half/pallas_call | solution.py:296
  47.9 0.5 collective-permute-start
  48.4 7.0 %collective-permute-done.other_ref = f32[64,32,512]{2,1,0:T(8,128)S(1)} collective-permute-done((f32[64,32,512]{2,1,0:T(8,128)}, f32[64,32,512]{2,1,0:T(8,128)S(1)}, u32[]{:S(2)}, u32[]{:S(2)}) %collective-permute-start) | collective-permute-done | bytes 4194336 | tf_op jit(solution)/shard_map/ppermute | solution.py:343
  55.4 0.0 copy-start
  55.4 2.0 %copy-done = f32[64,32,512]{2,1,0:T(8,128)} copy-done((f32[64,32,512]{2,1,0:T(8,128)}, f32[64,32,512]{2,1,0:T(8,128)S(1)}, u32[]{:S(2)}) %copy-start) | copy-done | bytes 4194328
  57.3 25.3 %second_half.1 = f32[32,32,256]{2,1,0:T(8,128)} custom-call(s32[4]{0:T(128)} %dil_ref.3, f32[64,32,512]{2,1,0:T(8,128)} %first_half.1.own_ref, f32[64,32,512]{2,1,0:T(8,128)} %copy-done, bf16[4,192,192]{2,1,0:T(8,128)(2,1)} %get-tuple-element.15.w_ref, f32[4,32,128]{2,1,0:T(8,128)} %get-tuple-element.16.bias_ref), custom_call_target="tpu_custom_call" | custom-call | tf_op jit(solution)/shard_map/second_half/pallas_call | solution.py:318
Async XLA Ops:
  47.9 7.5 %collective-permute-start = (f32[64,32,512]{2,1,0:T(8,128)}, f32[64,32,512]{2,1,0:T(8,128)S(1)}, u32[]{:S(2)}, u32[]{:S(2)}) collective-permute-start(f32[64,32,512]{2,1,0:T(8,128)} %first_half.1.own_ref), channel_id=1, source_target_pairs={{0,1},{1,0},{2,3},{3,2},{4,5},{5,4},{6,7},{7,6},{8,9},{9,8},{10,11... | collective-permute-start | bytes 12582920 | tf_op jit(solution)/shard_map/ppermute | solution.py:343
  55.4 2.0 %copy-start = (f32[64,32,512]{2,1,0:T(8,128)}, f32[64,32,512]{2,1,0:T(8,128)S(1)}, u32[]{:S(2)}) copy-start(f32[64,32,512]{2,1,0:T(8,128)S(1)} %collective-permute-done.other_ref) | copy-start | bytes 12582916

commit v3 on v2

v3 whole, which is shorter than its diff:
```python
import jax
import jax.numpy as jnp
from jax import lax
from jax.experimental import pallas as pl
from jax.experimental.pallas import tpu as pltpu
from jax.sharding import PartitionSpec as P

PC = 32
DIAGS = 128
HALF = 64
BAND = 32
BINW = 256
MAXDIL = 8
BINS = 8192
W1 = 512
W2 = 384
FW = 640
R = 96
PAD = 8
UNROLL = 16
ROWS = 32
MESH = pl.DeviceIdType.MESH


def split_store(y_ref, j, x):
    hi = x.astype(jnp.bfloat16)
    lo = (x - hi.astype(jnp.float32)).astype(jnp.bfloat16)
    y_ref[j, 0:PC, :] = hi
    y_ref[j, PC:2 * PC, :] = lo


def gather_taps(p, k, bias):
    width = p.shape[1]
    parts = [p[64 * b:64 * b + 32] + p[64 * b + 32:64 * b + 64] for b in range(3)]
    return (
        parts[1]
        + pltpu.roll(parts[0], k, 1)
        + pltpu.roll(parts[2], width - k, 1)
        + bias
    )


def valid_of(u, bins):
    low = jnp.maximum(0, HALF - u)
    high = jnp.where((u >= 0) & (u < DIAGS), jnp.minimum(BINS, BINS + HALF - u), 0)
    return (bins >= low) & (bins < high)


def conv(k, weights, bias, src, dst, v_ref, first_u, bins, start, count, n, last):
    width = bins.shape[1]
    cat = 2 if width % 256 else 1

    def group(base, rows):
        for g in range(0, rows, cat):
            stack = [
                jnp.concatenate([src[j - k], src[j], src[j + k]], axis=0)
                for j in [base + g + c + PAD for c in range(cat)]
            ]
            stack = stack[0] if cat == 1 else jnp.concatenate(stack, axis=1)
            p = jnp.dot(weights, stack, preferred_element_type=jnp.float32)
            for c in range(cat):
                j = base + g + c
                branch = gather_taps(p[:, c * width:(c + 1) * width], k, bias)
                branch = jnp.where(valid_of(first_u + j, bins), branch, 0.0)
                if n == 3:
                    last[0](j, v_ref[j] + branch)
                    continue
                if n == 1:
                    branch = v_ref[j] + branch
                    v_ref[j] = branch
                split_store(dst, j + PAD, jnp.maximum(branch, 0.0))

    def step(t, carry):
        group(start + t * UNROLL, UNROLL)
        if n == 3:
            last[1](t)
        return carry

    lax.fori_loop(0, count // UNROLL, step, 0)
    if count % UNROLL:
        group(start + count // UNROLL * UNROLL, count % UNROLL)


def blocks(dil_ref, first, w_ref, bias_ref, v_ref, ya, yb, first_u, bins, rows_of, last):
    for n in range(4):
        src, dst = (ya, yb) if n % 2 == 0 else (yb, ya)
        start, count = rows_of(n)
        bias = jnp.concatenate([bias_ref[first + n]] * (bins.shape[1] // 128), axis=1)
        conv(
            dil_ref[(first + n) // 2], w_ref[first + n], bias, src, dst, v_ref,
            first_u, bins, start, count, n, last,
        )


def trunk(dil_ref, feat_ref, del_ref, proj_ref, emb_ref, cw_ref, cb_ref, out_ref,
          kept, land, emb_land, w_ref, bias_ref, row_s, col_s, v_ref, ya, yb, m_ref, v2_ref, ya2, yb2, o_ref,
          send, recv, esend, erecv, msend, mrecv, osem):
    row = lax.axis_index("rows")
    band = lax.axis_index("band")
    near = [(row, lax.rem(band + d, 4)) for d in range(1, 4)]
    after = [(lax.rem(row + 1, ROWS), d) for d in range(4)]
    before = [(lax.rem(row + ROWS - 1, ROWS), d) for d in range(4)]
    barrier = pltpu.get_barrier_semaphore()
    for r, b in near + after + before:
        pl.semaphore_signal(barrier, inc=1, device_id={"rows": r, "band": b}, device_id_type=MESH)

    same = lax.broadcasted_iota(jnp.int32, (64, 64), 0) == lax.broadcasted_iota(jnp.int32, (64, 64), 1)
    gone = jnp.sum(jnp.where(same, del_ref[...].astype(jnp.float32), 0.0), axis=1, keepdims=True)
    kept[...] = (feat_ref[...].astype(jnp.float32) * (1.0 - gone)).astype(jnp.bfloat16)

    pl.semaphore_wait(barrier, 11)
    copies = []

    def send_to(r, b, slot, index):
        copies.append(pltpu.make_async_remote_copy(
            kept, land.at[pl.ds(256 * slot + 64 * band, 64)], send.at[index], recv.at[slot, band],
            device_id={"rows": r, "band": b}, device_id_type=MESH))

    for d, (r, b) in enumerate(near):
        send_to(r, b, 1, d)
    for d, (r, b) in enumerate(after):
        send_to(r, b, 0, 3 + d)
    for d, (r, b) in enumerate(before):
        send_to(r, b, 2, 7 + d)
    for d, (r, b) in enumerate(near):
        copies.append(pltpu.make_async_remote_copy(
            emb_ref, emb_land.at[band], esend.at[d], erecv.at[band],
            device_id={"rows": r, "band": b}, device_id_type=MESH))
    for copy in copies:
        copy.start()
    land[pl.ds(256 + 64 * band, 64), :] = kept[...]
    emb_land[band] = emb_ref[...]

    square = lax.broadcasted_iota(jnp.int32, (PC, PC), 0) == lax.broadcasted_iota(jnp.int32, (PC, PC), 1)

    def weights(n, carry):
        for b in range(3):
            t = [cw_ref[n, 3 * a + b] for a in range(3)]
            wide = jnp.concatenate([t[0], t[0], t[1], t[1], t[2], t[2]], axis=1)
            high = wide.astype(jnp.bfloat16)
            w_ref[n, 64 * b:64 * b + 32, :] = high
            w_ref[n, 64 * b + 32:64 * b + 64, :] = (wide - high.astype(jnp.float32)).astype(jnp.bfloat16)
        column = jnp.sum(jnp.where(square, cb_ref[n], 0.0), axis=1, keepdims=True)
        bias_ref[n] = jnp.broadcast_to(column, (PC, 128))
        return carry

    lax.fori_loop(0, 8, weights, 0)
    for y, width in ((ya, W1), (yb, W1), (ya2, W2), (yb2, W2)):
        zero = jnp.zeros((PAD, 2 * PC, width), jnp.bfloat16)
        y[0:PAD] = zero
        y[PAD + R:] = zero

    def arrived(buf, sem):
        pltpu.make_async_copy(buf, buf, sem).wait()

    for d in range(1, 4):
        b = lax.rem(band + d, 4)
        arrived(land.at[pl.ds(256 + 64 * b, 64)], recv.at[1, b])
        arrived(emb_land.at[b], erecv.at[b])
    for d in range(4):
        arrived(land.at[pl.ds(64 * d, 64)], recv.at[0, d])
        arrived(land.at[pl.ds(512 + 64 * d, 64)], recv.at[2, d])

    half = lax.rem(band, 2)
    pair = lax.div(band, 2)
    first_u = half * 32
    skip = 128 - 128 * pair
    bin0 = row * BINW - 160 + 64 * pair
    projected = lax.dot_general(
        proj_ref[...], land[pl.ds(32 + 64 * pair, FW), :], (((0,), (1,)), ((), ())),
        preferred_element_type=jnp.float32,
    )
    row_s[...] = projected[:PC, 64:64 + W1]
    col_s[...] = projected[PC:]
    bins = lax.broadcasted_iota(jnp.int32, (1, W1), 1) + bin0
    lanes = lax.broadcasted_iota(jnp.int32, (PC, BAND), 1)

    def start_rows(t, carry):
        for s in range(8):
            j = t * 8 + s
            u = first_u + j
            col = pltpu.roll(col_s[...], FW - u, 1)[:, :W1]
            emb = jnp.where(lanes == lax.rem(u, BAND), emb_land[lax.div(u, BAND)], 0.0)
            x = jnp.maximum(row_s[...] + col + jnp.sum(emb, axis=1, keepdims=True), 0.0)
            x = jnp.where(valid_of(u, bins), x, 0.0)
            v_ref[j] = x
            split_store(ya, j + PAD, x)
        return carry

    lax.fori_loop(0, R // 8, start_rows, 0)

    def swap(index, base):
        rows = m_ref.at[pl.ds(base, 16)]
        return pltpu.make_async_remote_copy(
            rows, rows, msend.at[index], mrecv.at[index],
            device_id={"rows": row, "band": band + 1 - 2 * half}, device_id_type=MESH)

    def keep(j, value):
        m_ref[first_u + j] = value

    def keep_done(t):
        swap(t, 64 * half + 16 * t).start()

    blocks(dil_ref, 0, w_ref, bias_ref, v_ref, ya, yb, first_u, bins,
           lambda n: (half * (8 * n + 8), 88 - 8 * n), (keep, keep_done))
    for t in range(4):
        swap(t, 64 * half + 16 * t).wait_send()
        swap(t, 64 - 64 * half + 16 * t).wait_recv()

    u2 = band * BAND - 32
    bins2 = lax.broadcasted_iota(jnp.int32, (1, W2), 1) + (bin0 + skip)

    def mirror_rows(t, carry):
        for s in range(8):
            j = t * 8 + s
            u = u2 + j
            ui = jnp.clip(u, 0, DIAGS - 1)
            own = m_ref[ui, :, pl.ds(pl.multiple_of(skip, 128), W2)]
            partner = m_ref[jnp.clip(DIAGS - u, 0, DIAGS - 1)]
            partner = pltpu.roll(partner, lax.rem(W1 + HALF - skip - ui + W1, W1), 1)[:, :W2]
            partner = jnp.where(u > 0, partner, 0.0)
            x = jnp.where(valid_of(u, bins2), 0.5 * (own + partner), 0.0)
            v2_ref[j] = x
            split_store(ya2, j + PAD, jnp.maximum(x, 0.0))
        return carry

    lax.fori_loop(0, R // 8, mirror_rows, 0)

    shift = W2 - 32 - 64 * pair

    def emit(j, value):
        o_ref[j - 32] = pltpu.roll(value, shift, 1)[:, :BINW]

    def out_copy(j):
        return pltpu.make_async_copy(o_ref.at[j], out_ref.at[:, j, :], osem.at[j])

    def emit_done(t):
        for r in range(16):
            out_copy(16 * t + r).start()

    blocks(dil_ref, 4, w_ref, bias_ref, v2_ref, ya2, yb2, u2, bins2,
           lambda n: (8 * n + 8, 80 - 16 * n), (emit, emit_done))
    for j in range(BAND):
        out_copy(j).wait()
    for copy in copies:
        copy.wait_send()


smem = pl.BlockSpec(memory_space=pltpu.SMEM)
vmem = pl.BlockSpec(memory_space=pltpu.VMEM)
hbm = pl.BlockSpec(memory_space=pl.ANY)
f32 = jnp.float32
bf16 = jnp.bfloat16


def body(features, deleted, proj_weight, distance_embed, conv_weight, conv_bias, dilations):
    dma = pltpu.SemaphoreType.DMA
    return pl.pallas_call(
        trunk,
        out_shape=jax.ShapeDtypeStruct((PC, BAND, BINW), f32),
        in_specs=[smem] + [vmem] * 6,
        out_specs=hbm,
        scratch_shapes=[
            pltpu.VMEM((64, 128), bf16),
            pltpu.VMEM((768, 128), bf16),
            pltpu.VMEM((4, PC, BAND), f32),
            pltpu.VMEM((8, 192, 192), bf16),
            pltpu.VMEM((8, PC, 128), f32),
            pltpu.VMEM((PC, W1), f32),
            pltpu.VMEM((PC, FW), f32),
            pltpu.VMEM((R, PC, W1), f32),
            pltpu.VMEM((R + 2 * PAD, 2 * PC, W1), bf16),
            pltpu.VMEM((R + 2 * PAD, 2 * PC, W1), bf16),
            pltpu.VMEM((DIAGS, PC, W1), f32),
            pltpu.VMEM((R, PC, W2), f32),
            pltpu.VMEM((R + 2 * PAD, 2 * PC, W2), bf16),
            pltpu.VMEM((R + 2 * PAD, 2 * PC, W2), bf16),
            pltpu.VMEM((BAND, PC, BINW), f32),
            dma((11,)), dma((3, 4)), dma((3,)), dma((4,)), dma((4,)), dma((4,)), dma((BAND,)),
        ],
        compiler_params=pltpu.CompilerParams(
            collective_id=0, has_side_effects=True, vmem_limit_bytes=58 * 2 ** 20),
        name="trunk",
    )(dilations, features, deleted.reshape(1, 64), proj_weight, distance_embed, conv_weight, conv_bias.reshape(8, 1, PC))


def solution(mesh):
    return jax.shard_map(
        body,
        mesh=mesh,
        in_specs=(
            P(("rows", "band"), None),
            P(("rows", "band")),
            P(),
            P(None, "band"),
            P(),
            P(),
            P(),
        ),
        out_specs=P(None, "band", "rows"),
        check_vma=False,
    )
```

time: 82.9 us -> 67.4 us (0.81)
  Pallas kernels: 71.8 us -> 63.5 us
  waiting for transfers between devices: 7 us -> 0 us
    pallas_call x3 -> x1, Pallas kernels: 71.8 us -> 63.5 us  [body(): pl.pallas_call(trunk, out_shape=jax.ShapeDtypeStruct((PC, BAND, BINW), f3...]
    ppermute x1 -> x0, waiting for transfers between devices: 7 us -> none  [body(): other = lax.ppermute(mine, 'band', [(0, 1), (1, 0), (2, 3), (3, 2)])]
    unnamed x3 -> x2, local copies, waits for them, and re-layouts: 3.41 us -> 3.74 us
  transfers between devices with their start and end apart: 1 -> 0, of which waited for: 1 -> 0; matrix products, arithmetic and copies ran while one was open for 0% -> 0% of each run, Pallas kernels for 0% -> 0%
where the time goes in v3:
time: 67.4 us; the launch traced here: 67.2 us
  Pallas kernels  63.5 us (94%)
  local copies, waits for them, and re-layouts  3.74 us (6%)
    pallas_call x1, Pallas kernels, body(): pl.pallas_call(trunk, out_shape=jax.ShapeDtypeStruct((PC, BAND, BINW), f3...  63.5 us
    unnamed x2, local copies, waits for them, and re-layouts  3.74 us

profile of v3, /device:TPU:1, one launch (start us, length us, event | category | flops | bytes accessed | tf_op | source)
XLA Modules:
  0.0 67.2 jit_solution(15267430663552668308)
XLA Ops:
  0.0 1.4 %copy.8.proj_ref = bf16[128,64]{1,0:T(8,128)(2,1)} copy(bf16[128,64]{0,1:T(8,128)(2,1)} %param.9) | data formatting | bytes 32768 | tf_op args[2]
  1.4 63.5 %trunk.1 = f32[32,32,256]{2,1,0:T(8,128)} custom-call(s32[4]{0:T(128)} %dil_ref.1, bf16[64,128]{1,0:T(8,128)(2,1)} %feat_ref.1, s32[1,64]{1,0:T(1,128)} %bitcast.3, bf16[128,64]{1,0:T(8,128)(2,1)} %copy.8.proj_ref, f32[32,32]{1,0:T(8,128)} %emb_ref.1, f32[8,9,32,32]{3,2,1,0:T(8,128)} %cw_ref.1, f32[8,1,32]{2,1,0:T(1,128)} %bitcast.2), custom_call_target="tpu_custom_call" | custom-call | tf_op jit(solution)/shard_map/trunk/pallas_call | solution.py:258
  64.9 2.3 %copy.10 = f32[32,32,256]{2,1,0:T(8,128)} copy(f32[32,32,256]{2,1,0:T(8,128)} %trunk.1) | data formatting | bytes 2097152

commit v4 on v3

v4 whole, which is shorter than its diff:
```python
import jax
import jax.numpy as jnp
from jax import lax
from jax.experimental import pallas as pl
from jax.experimental.pallas import tpu as pltpu
from jax.sharding import PartitionSpec as P

PC = 32
DIAGS = 128
HALF = 64
BAND = 32
BINW = 256
MAXDIL = 8
BINS = 8192
W1 = 512
W2 = 384
FW = 640
HALO = 8
R1 = 80
R2 = 72
ROWS = 32
MESH = pl.DeviceIdType.MESH


def split_store(y_ref, j, x):
    hi = x.astype(jnp.bfloat16)
    lo = (x - hi.astype(jnp.float32)).astype(jnp.bfloat16)
    y_ref[j, 0:PC, :] = hi
    y_ref[j, PC:2 * PC, :] = lo


def gather_taps(p, k, bias):
    width = p.shape[1]
    parts = [p[64 * b:64 * b + 32] + p[64 * b + 32:64 * b + 64] for b in range(3)]
    return (
        parts[1]
        + pltpu.roll(parts[0], k, 1)
        + pltpu.roll(parts[2], width - k, 1)
        + bias
    )


def valid_of(u, bins):
    low = jnp.maximum(0, HALF - u)
    high = jnp.where((u >= 0) & (u < DIAGS), jnp.minimum(BINS, BINS + HALF - u), 0)
    return (bins >= low) & (bins < high)


def conv_rows(ctx, base, count, sink):
    k, weights, bias, src, u0, bins = ctx
    width = bins.shape[1]
    cat = 2 if width % 256 else 1
    for g in range(0, count, cat):
        stack = [
            jnp.concatenate([src[q - k], src[q], src[q + k]], axis=0)
            for q in [base + g + c for c in range(cat)]
        ]
        stack = stack[0] if cat == 1 else jnp.concatenate(stack, axis=1)
        p = jnp.dot(weights, stack, preferred_element_type=jnp.float32)
        for c in range(cat):
            q = base + g + c
            branch = gather_taps(p[:, c * width:(c + 1) * width], k, bias)
            sink(q, jnp.where(valid_of(u0 + q, bins), branch, 0.0))


def trunk(dil_ref, feat_ref, del_ref, proj_ref, emb_ref, cw_ref, cb_ref, out_ref,
          kept, land, emb_land, w_ref, bias_ref, row_s, col_s, v_ref, ya, yb, m_ref, v2_ref, ya2, yb2, o_ref, halo1, halo2,
          send, recv, esend, erecv, msend, mrecv, hsend, hrecv, osem):
    row = lax.axis_index("rows")
    band = lax.axis_index("band")
    near = [(row, lax.rem(band + d, 4)) for d in range(1, 4)]
    after = [(lax.rem(row + 1, ROWS), d) for d in range(4)]
    before = [(lax.rem(row + ROWS - 1, ROWS), d) for d in range(4)]
    barrier = pltpu.get_barrier_semaphore()
    for r, b in near + after + before:
        pl.semaphore_signal(barrier, inc=1, device_id={"rows": r, "band": b}, device_id_type=MESH)

    same = lax.broadcasted_iota(jnp.int32, (64, 64), 0) == lax.broadcasted_iota(jnp.int32, (64, 64), 1)
    gone = jnp.sum(jnp.where(same, del_ref[...].astype(jnp.float32), 0.0), axis=1, keepdims=True)
    kept[...] = (feat_ref[...].astype(jnp.float32) * (1.0 - gone)).astype(jnp.bfloat16)

    pl.semaphore_wait(barrier, 11)
    copies = []

    def send_to(r, b, slot, index):
        copies.append(pltpu.make_async_remote_copy(
            kept, land.at[pl.ds(256 * slot + 64 * band, 64)], send.at[index], recv.at[slot, band],
            device_id={"rows": r, "band": b}, device_id_type=MESH))

    for d, (r, b) in enumerate(near):
        send_to(r, b, 1, d)
    for d, (r, b) in enumerate(after):
        send_to(r, b, 0, 3 + d)
    for d, (r, b) in enumerate(before):
        send_to(r, b, 2, 7 + d)
    for d, (r, b) in enumerate(near):
        copies.append(pltpu.make_async_remote_copy(
            emb_ref, emb_land.at[band], esend.at[d], erecv.at[band],
            device_id={"rows": r, "band": b}, device_id_type=MESH))
    for copy in copies:
        copy.start()
    land[pl.ds(256 + 64 * band, 64), :] = kept[...]
    emb_land[band] = emb_ref[...]

    square = lax.broadcasted_iota(jnp.int32, (PC, PC), 0) == lax.broadcasted_iota(jnp.int32, (PC, PC), 1)

    def weights(n, carry):
        for b in range(3):
            t = [cw_ref[n, 3 * a + b] for a in range(3)]
            wide = jnp.concatenate([t[0], t[0], t[1], t[1], t[2], t[2]], axis=1)
            high = wide.astype(jnp.bfloat16)
            w_ref[n, 64 * b:64 * b + 32, :] = high
            w_ref[n, 64 * b + 32:64 * b + 64, :] = (wide - high.astype(jnp.float32)).astype(jnp.bfloat16)
        column = jnp.sum(jnp.where(square, cb_ref[n], 0.0), axis=1, keepdims=True)
        bias_ref[n] = jnp.broadcast_to(column, (PC, 128))
        return carry

    lax.fori_loop(0, 8, weights, 0)
    zero = jnp.zeros((HALO, 2 * PC, W1), jnp.bfloat16)
    for y in (ya, yb):
        y[0:HALO] = zero
        y[R1 - HALO:] = zero

    def arrived(buf, sem):
        pltpu.make_async_copy(buf, buf, sem).wait()

    for d in range(1, 4):
        b = lax.rem(band + d, 4)
        arrived(land.at[pl.ds(256 + 64 * b, 64)], recv.at[1, b])
        arrived(emb_land.at[b], erecv.at[b])
    for d in range(4):
        arrived(land.at[pl.ds(64 * d, 64)], recv.at[0, d])
        arrived(land.at[pl.ds(512 + 64 * d, 64)], recv.at[2, d])

    half = lax.rem(band, 2)
    pair = lax.div(band, 2)
    other = band + 1 - 2 * half
    u0 = 64 * half - HALO
    skip = 128 - 128 * pair
    bin0 = row * BINW - 160 + 64 * pair
    projected = lax.dot_general(
        proj_ref[...], land[pl.ds(32 + 64 * pair, FW), :], (((1,), (1,)), ((), ())),
        preferred_element_type=jnp.float32,
    )
    row_s[...] = projected[:PC, 64:64 + W1]
    col_s[...] = projected[PC:]
    bins = lax.broadcasted_iota(jnp.int32, (1, W1), 1) + bin0
    lanes = lax.broadcasted_iota(jnp.int32, (PC, BAND), 1)

    def start_rows(t, carry):
        for s in range(24):
            q = HALO - HALO * half + t * 24 + s
            u = u0 + q
            col = pltpu.roll(col_s[...], FW - u, 1)[:, :W1]
            emb = jnp.where(lanes == lax.rem(u, BAND), emb_land[lax.div(u, BAND)], 0.0)
            x = jnp.maximum(row_s[...] + col + jnp.sum(emb, axis=1, keepdims=True), 0.0)
            x = jnp.where(valid_of(u, bins), x, 0.0)
            v_ref[q] = x
            split_store(ya, q, x)
        return carry

    lax.fori_loop(0, 3, start_rows, 0)

    def context(n, src, u0, bins):
        bias = jnp.concatenate([bias_ref[n]] * (bins.shape[1] // 128), axis=1)
        return dil_ref[n // 2], w_ref[n], bias, src, u0, bins

    def branch_to(v, dst, residual):
        def sink(q, value):
            if residual:
                value = v[q] + value
                v[q] = value
            split_store(dst, q, jnp.maximum(value, 0.0))
        return sink

    def to_other(src, dst, ssem, rsem):
        return pltpu.make_async_remote_copy(
            src, dst, ssem, rsem, device_id={"rows": row, "band": other}, device_id_type=MESH)

    def edge1(n, dst):
        edge = dst.at[pl.ds(64 - 56 * half, HALO)]
        return to_other(edge, halo1.at[n], hsend.at[n], hrecv.at[n])

    for n in range(3):
        src, dst = (ya, yb) if n % 2 == 0 else (yb, ya)
        if n:
            edge1(n - 1, src).wait()
            src[pl.ds(72 - 72 * half, HALO)] = halo1[n - 1]
        ctx = context(n, src, u0, bins)
        sink = branch_to(v_ref, dst, n == 1)

        def step(t, carry, n=n, dst=dst, ctx=ctx, sink=sink):
            conv_rows(ctx, HALO + half * (32 * t) + (1 - half) * (32 - 32 * t), 32, sink)

            @pl.when(t == 0)
            def _():
                edge1(n, dst).start()

            return carry

        lax.fori_loop(0, 2, step, 0)

    edge1(2, yb).wait()
    yb[pl.ds(72 - 72 * half, HALO)] = halo1[2]
    ctx3 = context(3, yb, u0, bins)

    def swap(t, core, count):
        at = 64 * core + (16 * t if count == 16 else 32) * pair + (48 - 16 * t if count == 16 else 20) * (1 - pair)
        rows = m_ref.at[pl.ds(at, count)]
        return to_other(rows, rows, msend.at[t], mrecv.at[t])

    def keep(q, value):
        m_ref[u0 + q] = v_ref[q] + value

    def last_step(t, carry):
        conv_rows(ctx3, HALO + 16 * t * pair + (48 - 16 * t) * (1 - pair), 16, keep)

        @pl.when(t < 2)
        def _():
            swap(t, half, 16).start()

        @pl.when(t == 2)
        def _():
            swap(2, half, 12).start()

        return carry

    lax.fori_loop(0, 4, last_step, 0)
    for t in range(3):
        count = 16 if t < 2 else 12
        swap(t, half, count).wait_send()
        swap(t, 1 - half, count).wait_recv()

    u2 = band * BAND - 32 + 24 * half
    bins2 = lax.broadcasted_iota(jnp.int32, (1, W2), 1) + (bin0 + skip)

    def mirror_rows(t, carry):
        for s in range(24):
            q = t * 24 + s
            u = u2 + q
            ui = jnp.clip(u, 0, DIAGS - 1)
            own = m_ref[ui, :, pl.ds(pl.multiple_of(skip, 128), W2)]
            partner = m_ref[jnp.clip(DIAGS - u, 0, DIAGS - 1)]
            partner = pltpu.roll(partner, lax.rem(W1 + HALF - skip - ui + W1, W1), 1)[:, :W2]
            partner = jnp.where(u > 0, partner, 0.0)
            x = jnp.where(valid_of(u, bins2), 0.5 * (own + partner), 0.0)
            v2_ref[q] = x
            split_store(ya2, q, jnp.maximum(x, 0.0))
        return carry

    lax.fori_loop(0, 3, mirror_rows, 0)

    def edge2(n, dst):
        edge = dst.at[pl.ds(56 - 48 * half, HALO)]
        return to_other(edge, halo2.at[n], hsend.at[3 + n], hrecv.at[3 + n])

    for n in range(3):
        src, dst = (ya2, yb2) if n % 2 == 0 else (yb2, ya2)
        if n:
            edge2(n - 1, src).wait()
            src[pl.ds(64 - 64 * half, HALO)] = halo2[n - 1]
        ctx = context(4 + n, src, u2, bins2)
        sink = branch_to(v2_ref, dst, n == 1)
        conv_rows(ctx, 32 - 24 * half, 32, sink)
        edge2(n, dst).start()
        conv_rows(ctx, (8 + 8 * n) * (1 - half) + 40 * half, 24 - 8 * n, sink)
    edge2(2, yb2).wait()
    yb2[pl.ds(64 - 64 * half, HALO)] = halo2[2]

    shift = W2 - 32 - 64 * pair
    first = 32 - 24 * half
    ctx7 = context(7, yb2, u2, bins2)

    def emit(q, value):
        o_ref[q - first] = pltpu.roll(v2_ref[q] + value, shift, 1)[:, :BINW]

    def out_copy(j):
        return pltpu.make_async_copy(o_ref.at[j], out_ref.at[:, j, :], osem.at[j])

    for t in range(2):
        conv_rows(ctx7, first + 16 * t, 16, emit)
        for r in range(16):
            out_copy(16 * t + r).start()
    for j in range(BAND):
        out_copy(j).wait()
    for copy in copies:
        copy.wait_send()


smem = pl.BlockSpec(memory_space=pltpu.SMEM)
vmem = pl.BlockSpec(memory_space=pltpu.VMEM)
hbm = pl.BlockSpec(memory_space=pl.ANY)
f32 = jnp.float32
bf16 = jnp.bfloat16


def body(features, deleted, proj_weight, distance_embed, conv_weight, conv_bias, dilations):
    dma = pltpu.SemaphoreType.DMA
    return pl.pallas_call(
        trunk,
        out_shape=jax.ShapeDtypeStruct((PC, BAND, BINW), f32),
        in_specs=[smem] + [vmem] * 6,
        out_specs=hbm,
        scratch_shapes=[
            pltpu.VMEM((64, 128), bf16),
            pltpu.VMEM((768, 128), bf16),
            pltpu.VMEM((4, PC, BAND), f32),
            pltpu.VMEM((8, 192, 192), bf16),
            pltpu.VMEM((8, PC, 128), f32),
            pltpu.VMEM((PC, W1), f32),
            pltpu.VMEM((PC, FW), f32),
            pltpu.VMEM((R1, PC, W1), f32),
            pltpu.VMEM((R1, 2 * PC, W1), bf16),
            pltpu.VMEM((R1, 2 * PC, W1), bf16),
            pltpu.VMEM((DIAGS, PC, W1), f32),
            pltpu.VMEM((R2, PC, W2), f32),
            pltpu.VMEM((R2, 2 * PC, W2), bf16),
            pltpu.VMEM((R2, 2 * PC, W2), bf16),
            pltpu.VMEM((BAND, PC, BINW), f32),
            pltpu.VMEM((3, HALO, 2 * PC, W1), bf16),
            pltpu.VMEM((3, HALO, 2 * PC, W2), bf16),
            dma((11,)), dma((3, 4)), dma((3,)), dma((4,)), dma((3,)), dma((3,)), dma((6,)), dma((6,)), dma((BAND,)),
        ],
        compiler_params=pltpu.CompilerParams(
            collective_id=0, has_side_effects=True, vmem_limit_bytes=58 * 2 ** 20),
        name="trunk",
    )(dilations, features, deleted.reshape(1, 64), proj_weight.T, distance_embed, conv_weight, conv_bias.reshape(8, 1, PC))


def solution(mesh):
    return jax.shard_map(
        body,
        mesh=mesh,
        in_specs=(
            P(("rows", "band"), None),
            P(("rows", "band")),
            P(),
            P(None, "band"),
            P(),
            P(),
            P(),
        ),
        out_specs=P(None, "band", "rows"),
        check_vma=False,
    )
```

time: 67.4 us -> 54.6 us (0.81)
  Pallas kernels: 63.5 us -> 52.1 us
  local copies, waits for them, and re-layouts: 3.74 us -> 2.31 us
    pallas_call x1, Pallas kernels: 63.5 us -> 52.1 us  [body(): pl.pallas_call(trunk, out_shape=jax.ShapeDtypeStruct((PC, BAND, BINW), f3...]
    unnamed x2 -> x1, local copies, waits for them, and re-layouts: 3.74 us -> 2.31 us
where the time goes in v4:
time: 54.6 us; the launch traced here: 54.4 us
  Pallas kernels  52.1 us (95%)
  local copies, waits for them, and re-layouts  2.31 us (4%)
    pallas_call x1, Pallas kernels, body(): pl.pallas_call(trunk, out_shape=jax.ShapeDtypeStruct((PC, BAND, BINW), f3...  52.1 us
    unnamed x1, local copies, waits for them, and re-layouts  2.31 us

profile of v4, /device:TPU:1, one launch (start us, length us, event | category | flops | bytes accessed | tf_op | source)
XLA Modules:
  0.0 54.4 jit_solution(80744035406755430)
XLA Ops:
  0.0 52.1 %trunk.1 = f32[32,32,256]{2,1,0:T(8,128)} custom-call(s32[4]{0:T(128)} %dil_ref.1, bf16[64,128]{1,0:T(8,128)(2,1)} %feat_ref.1, s32[1,64]{1,0:T(1,128)} %bitcast.5, bf16[64,128]{1,0:T(8,128)(2,1)} %bitcast.3, f32[32,32]{1,0:T(8,128)} %emb_ref.1, f32[8,9,32,32]{3,2,1,0:T(8,128)} %cw_ref.1, f32[8,1,32]{2,1,0:T(1,128)} %bitcast.4), custom_call_target="tpu_custom_call" | custom-call | tf_op jit(solution)/shard_map/trunk/pallas_call | solution.py:299
  52.1 2.3 %copy.9 = f32[32,32,256]{2,1,0:T(8,128)} copy(f32[32,32,256]{2,1,0:T(8,128)} %trunk.1) | data formatting | bytes 2097152

commit v5 on v4

--- a/solution.py
+++ b/solution.py
@@ -14,7 +14,7 @@
 BINS = 8192
 W1 = 512
 W2 = 384
-FW = 640
+FW = 512
 HALO = 8
 R1 = 80
 R2 = 72
@@ -63,44 +63,77 @@
             sink(q, jnp.where(valid_of(u0 + q, bins), branch, 0.0))
 
 
-def trunk(dil_ref, feat_ref, del_ref, proj_ref, emb_ref, cw_ref, cb_ref, out_ref,
-          kept, land, emb_land, w_ref, bias_ref, row_s, col_s, v_ref, ya, yb, m_ref, v2_ref, ya2, yb2, o_ref, halo1, halo2,
-          send, recv, esend, erecv, msend, mrecv, hsend, hrecv, osem):
+def trunk(dil_ref, feat_ref, del_ref, proj_ref, emb_ref, cw_hbm, cb_ref, out_ref,
+          kept, land, emb_land, cw_ref, w_ref, bias_ref, row_s, col_s, v_ref, ya, yb, m_ref, v2_ref, ya2, yb2, o_ref, halo1, halo2,
+          cw_sem, send, recv, esend, erecv, msend, mrecv, hsend, hrecv, osem):
     row = lax.axis_index("rows")
     band = lax.axis_index("band")
+    weights_in = pltpu.make_async_copy(cw_hbm, cw_ref, cw_sem)
+    weights_in.start()
     near = [(row, lax.rem(band + d, 4)) for d in range(1, 4)]
-    after = [(lax.rem(row + 1, ROWS), d) for d in range(4)]
-    before = [(lax.rem(row + ROWS - 1, ROWS), d) for d in range(4)]
+    upper = lax.div(band, 2)
+    far_row = jnp.clip(row + 2 * upper - 1, 0, ROWS - 1)
+    far = far_row != row
     barrier = pltpu.get_barrier_semaphore()
-    for r, b in near + after + before:
+
+    def greet(r, b):
         pl.semaphore_signal(barrier, inc=1, device_id={"rows": r, "band": b}, device_id_type=MESH)
+
+    for r, b in near:
+        greet(r, b)
+
+    @pl.when(row > 0)
+    def _():
+        greet(row - 1, 2)
+        greet(row - 1, 3)
+
+    @pl.when(row < ROWS - 1)
+    def _():
+        greet(row + 1, 0)
+        greet(row + 1, 1)
 
     same = lax.broadcasted_iota(jnp.int32, (64, 64), 0) == lax.broadcasted_iota(jnp.int32, (64, 64), 1)
     gone = jnp.sum(jnp.where(same, del_ref[...].astype(jnp.float32), 0.0), axis=1, keepdims=True)
     kept[...] = (feat_ref[...].astype(jnp.float32) * (1.0 - gone)).astype(jnp.bfloat16)
 
-    pl.semaphore_wait(barrier, 11)
-    copies = []
-
-    def send_to(r, b, slot, index):
-        copies.append(pltpu.make_async_remote_copy(
-            kept, land.at[pl.ds(256 * slot + 64 * band, 64)], send.at[index], recv.at[slot, band],
-            device_id={"rows": r, "band": b}, device_id_type=MESH))
+    pl.semaphore_wait(barrier, jnp.where(far, 7, 3))
+
+    def slot(i):
+        return land.at[pl.ds(64 * i, 64)]
+
+    def send_to(r, b, to, index):
+        return pltpu.make_async_remote_copy(
+            kept, slot(to), send.at[index], recv.at[to],
+            device_id={"rows": r, "band": b}, device_id_type=MESH)
+
+    def send_far(d):
+        return send_to(far_row, d, lax.rem(band + 6, 8), 3 + d)
+
+    def send_emb(d, r, b):
+        return pltpu.make_async_remote_copy(
+            emb_ref, emb_land.at[band], esend.at[d], erecv.at[band],
+            device_id={"rows": r, "band": b}, device_id_type=MESH)
+
+    @pl.when(far)
+    def _():
+        for d in range(4):
+            send_far(d).start()
 
     for d, (r, b) in enumerate(near):
-        send_to(r, b, 1, d)
-    for d, (r, b) in enumerate(after):
-        send_to(r, b, 0, 3 + d)
-    for d, (r, b) in enumerate(before):
-        send_to(r, b, 2, 7 + d)
+        send_to(r, b, 2 + band, d).start()
     for d, (r, b) in enumerate(near):
-        copies.append(pltpu.make_async_remote_copy(
-            emb_ref, emb_land.at[band], esend.at[d], erecv.at[band],
-            device_id={"rows": r, "band": b}, device_id_type=MESH))
-    for copy in copies:
-        copy.start()
-    land[pl.ds(256 + 64 * band, 64), :] = kept[...]
+        send_emb(d, r, b).start()
+    land[pl.ds(128 + 64 * band, 64), :] = kept[...]
     emb_land[band] = emb_ref[...]
+    none = jnp.zeros((128, 128), jnp.bfloat16)
+
+    @pl.when(row == 0)
+    def _():
+        land[0:128] = none
+
+    @pl.when(row == ROWS - 1)
+    def _():
+        land[384:512] = none
 
     square = lax.broadcasted_iota(jnp.int32, (PC, PC), 0) == lax.broadcasted_iota(jnp.int32, (PC, PC), 1)
 
@@ -115,6 +148,7 @@
         bias_ref[n] = jnp.broadcast_to(column, (PC, 128))
         return carry
 
+    weights_in.wait()
     lax.fori_loop(0, 8, weights, 0)
     zero = jnp.zeros((HALO, 2 * PC, W1), jnp.bfloat16)
     for y in (ya, yb):
@@ -126,11 +160,18 @@
 
     for d in range(1, 4):
         b = lax.rem(band + d, 4)
-        arrived(land.at[pl.ds(256 + 64 * b, 64)], recv.at[1, b])
+        arrived(slot(2 + b), recv.at[2 + b])
         arrived(emb_land.at[b], erecv.at[b])
-    for d in range(4):
-        arrived(land.at[pl.ds(64 * d, 64)], recv.at[0, d])
-        arrived(land.at[pl.ds(512 + 64 * d, 64)], recv.at[2, d])
+
+    @pl.when(row > 0)
+    def _():
+        for i in (0, 1):
+            arrived(slot(i), recv.at[i])
+
+    @pl.when(row < ROWS - 1)
+    def _():
+        for i in (6, 7):
+            arrived(slot(i), recv.at[i])
 
     half = lax.rem(band, 2)
     pair = lax.div(band, 2)
@@ -139,10 +180,9 @@
     skip = 128 - 128 * pair
     bin0 = row * BINW - 160 + 64 * pair
     projected = lax.dot_general(
-        proj_ref[...], land[pl.ds(32 + 64 * pair, FW), :], (((1,), (1,)), ((), ())),
-        preferred_element_type=jnp.float32,
+        proj_ref[...], land[...], (((1,), (1,)), ((), ())), preferred_element_type=jnp.float32
     )
-    row_s[...] = projected[:PC, 64:64 + W1]
+    row_s[...] = pltpu.roll(projected[:PC], 32 + (W1 - 64) * pair, 1)
     col_s[...] = projected[PC:]
     bins = lax.broadcasted_iota(jnp.int32, (1, W1), 1) + bin0
     lanes = lax.broadcasted_iota(jnp.int32, (PC, BAND), 1)
@@ -151,7 +191,7 @@
         for s in range(24):
             q = HALO - HALO * half + t * 24 + s
             u = u0 + q
-            col = pltpu.roll(col_s[...], FW - u, 1)[:, :W1]
+            col = pltpu.roll(col_s[...], lax.rem(2 * W1 + 96 - 64 * pair - u, W1), 1)
             emb = jnp.where(lanes == lax.rem(u, BAND), emb_land[lax.div(u, BAND)], 0.0)
             x = jnp.maximum(row_s[...] + col + jnp.sum(emb, axis=1, keepdims=True), 0.0)
             x = jnp.where(valid_of(u, bins), x, 0.0)
@@ -226,17 +266,12 @@
         return carry
 
     lax.fori_loop(0, 4, last_step, 0)
-    for t in range(3):
-        count = 16 if t < 2 else 12
-        swap(t, half, count).wait_send()
-        swap(t, 1 - half, count).wait_recv()
-
     u2 = band * BAND - 32 + 24 * half
     bins2 = lax.broadcasted_iota(jnp.int32, (1, W2), 1) + (bin0 + skip)
 
-    def mirror_rows(t, carry):
-        for s in range(24):
-            q = t * 24 + s
+    def mirror_rows(start):
+        for s in range(8):
+            q = start + s
             u = u2 + q
             ui = jnp.clip(u, 0, DIAGS - 1)
             own = m_ref[ui, :, pl.ds(pl.multiple_of(skip, 128), W2)]
@@ -246,26 +281,40 @@
             x = jnp.where(valid_of(u, bins2), 0.5 * (own + partner), 0.0)
             v2_ref[q] = x
             split_store(ya2, q, jnp.maximum(x, 0.0))
-        return carry
-
-    lax.fori_loop(0, 3, mirror_rows, 0)
+
+    ready = (((24, 32), (32, 40), (40, 48)), ((8, 16), (16, 24), (48, 56), (56, 64)), ((0, 0), (64, 8)))
+    for t in range(3):
+        swap(t, 1 - half, 16 if t < 2 else 12).wait_recv()
+        for low, high in ready[t]:
+            mirror_rows(low + (high - low) * half)
+    for t in range(3):
+        swap(t, half, 16 if t < 2 else 12).wait_send()
 
     def edge2(n, dst):
         edge = dst.at[pl.ds(56 - 48 * half, HALO)]
         return to_other(edge, halo2.at[n], hsend.at[3 + n], hrecv.at[3 + n])
 
-    for n in range(3):
-        src, dst = (ya2, yb2) if n % 2 == 0 else (yb2, ya2)
-        if n:
-            edge2(n - 1, src).wait()
-            src[pl.ds(64 - 64 * half, HALO)] = halo2[n - 1]
-        ctx = context(4 + n, src, u2, bins2)
-        sink = branch_to(v2_ref, dst, n == 1)
-        conv_rows(ctx, 32 - 24 * half, 32, sink)
-        edge2(n, dst).start()
-        conv_rows(ctx, (8 + 8 * n) * (1 - half) + 40 * half, 24 - 8 * n, sink)
-    edge2(2, yb2).wait()
-    yb2[pl.ds(64 - 64 * half, HALO)] = halo2[2]
+    def land2(n, y):
+        edge2(n, y).wait()
+        y[pl.ds(64 - 64 * half, HALO)] = halo2[n]
+
+    def rows2(ctx, low, high, count, sink):
+        conv_rows(ctx, low + (high - low) * half, count, sink)
+
+    ctx, sink = context(4, ya2, u2, bins2), branch_to(v2_ref, yb2, False)
+    rows2(ctx, 40, 8, 24, sink)
+    edge2(0, yb2).start()
+    rows2(ctx, 8, 32, 32, sink)
+    ctx, sink = context(5, yb2, u2, bins2), branch_to(v2_ref, ya2, True)
+    rows2(ctx, 16, 24, 32, sink)
+    land2(0, yb2)
+    rows2(ctx, 48, 8, 16, sink)
+    edge2(1, ya2).start()
+    ctx, sink = context(6, ya2, u2, bins2), branch_to(v2_ref, yb2, False)
+    rows2(ctx, 24, 24, 24, sink)
+    land2(1, ya2)
+    rows2(ctx, 48, 8, 16, sink)
+    edge2(2, yb2).start()
 
     shift = W2 - 32 - 64 * pair
     first = 32 - 24 * half
@@ -277,14 +326,24 @@
     def out_copy(j):
         return pltpu.make_async_copy(o_ref.at[j], out_ref.at[:, j, :], osem.at[j])
 
-    for t in range(2):
-        conv_rows(ctx7, first + 16 * t, 16, emit)
-        for r in range(16):
-            out_copy(16 * t + r).start()
+    def finish(low, high, count):
+        rows2(ctx7, low, high, count, emit)
+        for r in range(count):
+            out_copy(low + (high - low) * half - first + r).start()
+
+    finish(32, 16, 24)
+    land2(2, yb2)
+    finish(56, 8, 8)
     for j in range(BAND):
         out_copy(j).wait()
-    for copy in copies:
-        copy.wait_send()
+    for d, (r, b) in enumerate(near):
+        send_to(r, b, 2 + band, d).wait_send()
+        send_emb(d, r, b).wait_send()
+
+    @pl.when(far)
+    def _():
+        for d in range(4):
+            send_far(d).wait_send()
 
 
 smem = pl.BlockSpec(memory_space=pltpu.SMEM)
@@ -299,12 +358,13 @@
     return pl.pallas_call(
         trunk,
         out_shape=jax.ShapeDtypeStruct((PC, BAND, BINW), f32),
-        in_specs=[smem] + [vmem] * 6,
+        in_specs=[smem] + [vmem] * 4 + [hbm, vmem],
         out_specs=hbm,
         scratch_shapes=[
             pltpu.VMEM((64, 128), bf16),
-            pltpu.VMEM((768, 128), bf16),
+            pltpu.VMEM((FW, 128), bf16),
             pltpu.VMEM((4, PC, BAND), f32),
+            pltpu.VMEM((8, 9, PC, PC), f32),
             pltpu.VMEM((8, 192, 192), bf16),
             pltpu.VMEM((8, PC, 128), f32),
             pltpu.VMEM((PC, W1), f32),
@@ -319,10 +379,10 @@
             pltpu.VMEM((BAND, PC, BINW), f32),
             pltpu.VMEM((3, HALO, 2 * PC, W1), bf16),
             pltpu.VMEM((3, HALO, 2 * PC, W2), bf16),
-            dma((11,)), dma((3, 4)), dma((3,)), dma((4,)), dma((3,)), dma((3,)), dma((6,)), dma((6,)), dma((BAND,)),
+            dma, dma((7,)), dma((8,)), dma((3,)), dma((4,)), dma((3,)), dma((3,)), dma((6,)), dma((6,)), dma((BAND,)),
         ],
         compiler_params=pltpu.CompilerParams(
-            collective_id=0, has_side_effects=True, vmem_limit_bytes=58 * 2 ** 20),
+            collective_id=0, has_side_effects=True, vmem_limit_bytes=46 * 2 ** 20),
         name="trunk",
     )(dilations, features, deleted.reshape(1, 64), proj_weight.T, distance_embed, conv_weight, conv_bias.reshape(8, 1, PC))
 

time: 54.6 us -> 50.1 us (0.918)
  Pallas kernels: 52.1 us -> 43.3 us
  local copies, waits for them, and re-layouts: 2.31 us -> 6.39 us
    pallas_call x1, Pallas kernels: 52.1 us -> 43.3 us  [body(): pl.pallas_call(trunk, out_shape=jax.ShapeDtypeStruct((PC, BAND, BINW), f3...]
    unnamed x1 -> x15, local copies, waits for them, and re-layouts: 2.31 us -> 6.39 us
where the time goes in v5:
time: 50.1 us; the launch traced here: 49.7 us
  Pallas kernels  43.3 us (86%)
  local copies, waits for them, and re-layouts  6.39 us (13%)
    pallas_call x1, Pallas kernels, body(): pl.pallas_call(trunk, out_shape=jax.ShapeDtypeStruct((PC, BAND, BINW), f3...  43.3 us
    unnamed x15, local copies, waits for them, and re-layouts  6.39 us

profile of v5, /device:TPU:1, one launch (start us, length us, event | category | flops | bytes accessed | tf_op | source)
XLA Modules:
  0.0 49.7 jit_solution(4477579543755162827)
XLA Ops:
  0.0 0.0 copy-start
  0.0 1.3 %copy-done = f32[8,9,32,32]{3,2,1,0:T(8,128)S(1)} copy-done((f32[8,9,32,32]{3,2,1,0:T(8,128)S(1)}, f32[8,9,32,32]{3,2,1,0:T(8,128)}, u32[]{:S(2)}) %copy-start) | copy-done | bytes 294936
  1.3 0.0 copy-start.1
  1.3 0.7 %copy-done.1 = bf16[64,128]{1,0:T(8,128)(2,1)S(1)} copy-done((bf16[64,128]{1,0:T(8,128)(2,1)S(1)}, bf16[64,128]{1,0:T(8,128)(2,1)}, u32[]{:S(2)}) %copy-start.1) | copy-done | bytes 16408
  2.0 0.0 copy-start.2
  2.0 0.7 %copy-done.2 = bf16[128,64]{0,1:T(8,128)(2,1)S(1)} copy-done((bf16[128,64]{0,1:T(8,128)(2,1)S(1)}, bf16[128,64]{0,1:T(8,128)(2,1)}, u32[]{:S(2)}) %copy-start.2) | copy-done | bytes 16408
  2.7 0.0 copy-start.3
  2.7 0.7 %copy-done.3 = f32[32,32]{1,0:T(8,128)S(1)} copy-done((f32[32,32]{1,0:T(8,128)S(1)}, f32[32,32]{1,0:T(8,128)}, u32[]{:S(2)}) %copy-start.3) | copy-done | bytes 4120
  3.4 0.0 copy-start.4
  3.4 0.7 %copy-done.4 = f32[8,32]{1,0:T(8,128)S(1)} copy-done((f32[8,32]{1,0:T(8,128)S(1)}, f32[8,32]{1,0:T(8,128)}, u32[]{:S(2)}) %copy-start.4) | copy-done | bytes 1048
  4.1 0.0 copy-start.5
  4.1 0.7 %copy-done.5 = s32[4]{0:T(128)S(1)} copy-done((s32[4]{0:T(128)S(1)}, s32[4]{0:T(128)}, u32[]{:S(2)}) %copy-start.5) | copy-done | bytes 40
  4.8 0.0 copy-start.6
  4.8 0.7 %copy-done.6 = s32[64]{0:T(128)S(1)} copy-done((s32[64]{0:T(128)S(1)}, s32[64]{0:T(128)}, u32[]{:S(2)}) %copy-start.6) | copy-done | bytes 280
  5.4 43.3 %trunk.1 = f32[32,32,256]{2,1,0:T(8,128)S(1)} custom-call(s32[4]{0:T(128)S(1)} %copy-done.5, bf16[64,128]{1,0:T(8,128)(2,1)S(1)} %copy-done.1, s32[1,64]{1,0:T(1,128)S(1)} %bitcast.5, bf16[64,128]{1,0:T(8,128)(2,1)S(1)} %bitcast.3, f32[32,32]{1,0:T(8,128)S(1)} %copy-done.3, f32[8,9,32,32]{3,2,1,0:T(8,128)S(1)} %copy-done, f32[8,1,32]{2,1,0:T(1,128)S(1)} %bitcast.4), custom_call_target="tpu_custom_call" | custom-call | tf_op jit(solution)/shard_map/trunk/pallas_call | solution.py:358
  48.7 1.0 %copy.9 = f32[32,32,256]{2,1,0:T(8,128)} copy(f32[32,32,256]{2,1,0:T(8,128)S(1)} %trunk.1) | data formatting | bytes 2097152
Async XLA Ops:
  0.0 1.3 %copy-start = (f32[8,9,32,32]{3,2,1,0:T(8,128)S(1)}, f32[8,9,32,32]{3,2,1,0:T(8,128)}, u32[]{:S(2)}) copy-start(f32[8,9,32,32]{3,2,1,0:T(8,128)} %cw_hbm.1) | copy-start | bytes 884740
  1.3 0.7 %copy-start.1 = (bf16[64,128]{1,0:T(8,128)(2,1)S(1)}, bf16[64,128]{1,0:T(8,128)(2,1)}, u32[]{:S(2)}) copy-start(bf16[64,128]{1,0:T(8,128)(2,1)} %feat_ref.1) | copy-start | bytes 49156
  2.0 0.7 %copy-start.2 = (bf16[128,64]{0,1:T(8,128)(2,1)S(1)}, bf16[128,64]{0,1:T(8,128)(2,1)}, u32[]{:S(2)}) copy-start(bf16[128,64]{0,1:T(8,128)(2,1)} %param.9) | copy-start | bytes 49156
  2.7 0.7 %copy-start.3 = (f32[32,32]{1,0:T(8,128)S(1)}, f32[32,32]{1,0:T(8,128)}, u32[]{:S(2)}) copy-start(f32[32,32]{1,0:T(8,128)} %emb_ref.1) | copy-start | bytes 12292
  3.4 0.7 %copy-start.4 = (f32[8,32]{1,0:T(8,128)S(1)}, f32[8,32]{1,0:T(8,128)}, u32[]{:S(2)}) copy-start(f32[8,32]{1,0:T(8,128)} %param.12) | copy-start | bytes 3076
  4.1 0.7 %copy-start.5 = (s32[4]{0:T(128)S(1)}, s32[4]{0:T(128)}, u32[]{:S(2)}) copy-start(s32[4]{0:T(128)} %dil_ref.1) | copy-start | bytes 52
  4.8 0.7 %copy-start.6 = (s32[64]{0:T(128)S(1)}, s32[64]{0:T(128)}, u32[]{:S(2)}) copy-start(s32[64]{0:T(128)} %param.8) | copy-start | bytes 772

commit v6 on v5

--- a/solution.py
+++ b/solution.py
@@ -63,13 +63,16 @@
             sink(q, jnp.where(valid_of(u0 + q, bins), branch, 0.0))
 
 
-def trunk(dil_ref, feat_ref, del_ref, proj_ref, emb_ref, cw_hbm, cb_ref, out_ref,
-          kept, land, emb_land, cw_ref, w_ref, bias_ref, row_s, col_s, v_ref, ya, yb, m_ref, v2_ref, ya2, yb2, o_ref, halo1, halo2,
-          cw_sem, send, recv, esend, erecv, msend, mrecv, hsend, hrecv, osem):
+def trunk(dil_ref, feat_in, del_in, proj_in, emb_in, cw_in, cb_in, out_ref,
+          feat_ref, del_ref, proj_ref, emb_ref, cw_ref, cb_ref, in_sem,
+          kept, land, emb_land, w_ref, bias_ref, row_s, col_s, v_ref, ya, yb, m_ref, v2_ref, ya2, yb2, o_ref, halo1, halo2,
+          send, recv, esend, erecv, msend, mrecv, hsend, hrecv, osem):
     row = lax.axis_index("rows")
     band = lax.axis_index("band")
-    weights_in = pltpu.make_async_copy(cw_hbm, cw_ref, cw_sem)
-    weights_in.start()
+    arguments = ((feat_in, feat_ref), (del_in, del_ref), (emb_in, emb_ref), (proj_in, proj_ref), (cb_in, cb_ref), (cw_in, cw_ref))
+    fetch = [pltpu.make_async_copy(src, dst, in_sem.at[i]) for i, (src, dst) in enumerate(arguments)]
+    for copy in fetch:
+        copy.start()
     near = [(row, lax.rem(band + d, 4)) for d in range(1, 4)]
     upper = lax.div(band, 2)
     far_row = jnp.clip(row + 2 * upper - 1, 0, ROWS - 1)
@@ -92,10 +95,13 @@
         greet(row + 1, 0)
         greet(row + 1, 1)
 
+    fetch[0].wait()
+    fetch[1].wait()
     same = lax.broadcasted_iota(jnp.int32, (64, 64), 0) == lax.broadcasted_iota(jnp.int32, (64, 64), 1)
     gone = jnp.sum(jnp.where(same, del_ref[...].astype(jnp.float32), 0.0), axis=1, keepdims=True)
     kept[...] = (feat_ref[...].astype(jnp.float32) * (1.0 - gone)).astype(jnp.bfloat16)
 
+    fetch[2].wait()
     pl.semaphore_wait(barrier, jnp.where(far, 7, 3))
 
     def slot(i):
@@ -148,7 +154,8 @@
         bias_ref[n] = jnp.broadcast_to(column, (PC, 128))
         return carry
 
-    weights_in.wait()
+    for copy in fetch[3:]:
+        copy.wait()
     lax.fori_loop(0, 8, weights, 0)
     zero = jnp.zeros((HALO, 2 * PC, W1), jnp.bfloat16)
     for y in (ya, yb):
@@ -192,7 +199,7 @@
             q = HALO - HALO * half + t * 24 + s
             u = u0 + q
             col = pltpu.roll(col_s[...], lax.rem(2 * W1 + 96 - 64 * pair - u, W1), 1)
-            emb = jnp.where(lanes == lax.rem(u, BAND), emb_land[lax.div(u, BAND)], 0.0)
+            emb = jnp.where(lanes == (u & 31), emb_land[u >> 5], 0.0)
             x = jnp.maximum(row_s[...] + col + jnp.sum(emb, axis=1, keepdims=True), 0.0)
             x = jnp.where(valid_of(u, bins), x, 0.0)
             v_ref[q] = x
@@ -229,16 +236,9 @@
         ctx = context(n, src, u0, bins)
         sink = branch_to(v_ref, dst, n == 1)
 
-        def step(t, carry, n=n, dst=dst, ctx=ctx, sink=sink):
-            conv_rows(ctx, HALO + half * (32 * t) + (1 - half) * (32 - 32 * t), 32, sink)
-
-            @pl.when(t == 0)
-            def _():
-                edge1(n, dst).start()
-
-            return carry
-
-        lax.fori_loop(0, 2, step, 0)
+        conv_rows(ctx, 40 - 32 * half, 32, sink)
+        edge1(n, dst).start()
+        conv_rows(ctx, 8 + 32 * half, 32, sink)
 
     edge1(2, yb).wait()
     yb[pl.ds(72 - 72 * half, HALO)] = halo1[2]
@@ -347,7 +347,6 @@
 
 
 smem = pl.BlockSpec(memory_space=pltpu.SMEM)
-vmem = pl.BlockSpec(memory_space=pltpu.VMEM)
 hbm = pl.BlockSpec(memory_space=pl.ANY)
 f32 = jnp.float32
 bf16 = jnp.bfloat16
@@ -357,14 +356,20 @@
     dma = pltpu.SemaphoreType.DMA
     return pl.pallas_call(
         trunk,
-        out_shape=jax.ShapeDtypeStruct((PC, BAND, BINW), f32),
-        in_specs=[smem] + [vmem] * 4 + [hbm, vmem],
+        out_shape=pltpu.VMEM((PC, BAND, BINW), f32),
+        in_specs=[smem] + [pl.BlockSpec(memory_space=pltpu.HBM)] * 6,
         out_specs=hbm,
         scratch_shapes=[
             pltpu.VMEM((64, 128), bf16),
+            pltpu.VMEM((1, 64), jnp.int32),
+            pltpu.VMEM((2 * PC, 128), bf16),
+            pltpu.VMEM((PC, BAND), f32),
+            pltpu.VMEM((8, 9, PC, PC), f32),
+            pltpu.VMEM((8, 1, PC), f32),
+            dma((6,)),
+            pltpu.VMEM((64, 128), bf16),
             pltpu.VMEM((FW, 128), bf16),
             pltpu.VMEM((4, PC, BAND), f32),
-            pltpu.VMEM((8, 9, PC, PC), f32),
             pltpu.VMEM((8, 192, 192), bf16),
             pltpu.VMEM((8, PC, 128), f32),
             pltpu.VMEM((PC, W1), f32),
@@ -379,10 +384,10 @@
             pltpu.VMEM((BAND, PC, BINW), f32),
             pltpu.VMEM((3, HALO, 2 * PC, W1), bf16),
             pltpu.VMEM((3, HALO, 2 * PC, W2), bf16),
-            dma, dma((7,)), dma((8,)), dma((3,)), dma((4,)), dma((3,)), dma((3,)), dma((6,)), dma((6,)), dma((BAND,)),
+            dma((7,)), dma((8,)), dma((3,)), dma((4,)), dma((3,)), dma((3,)), dma((6,)), dma((6,)), dma((BAND,)),
         ],
         compiler_params=pltpu.CompilerParams(
-            collective_id=0, has_side_effects=True, vmem_limit_bytes=46 * 2 ** 20),
+            collective_id=0, has_side_effects=True, vmem_limit_bytes=55 * 2 ** 20),
         name="trunk",
     )(dilations, features, deleted.reshape(1, 64), proj_weight.T, distance_embed, conv_weight, conv_bias.reshape(8, 1, PC))
 

time: 50.1 us -> 44.8 us (0.89)
  local copies, waits for them, and re-layouts: 6.39 us -> 0.97 us
    unnamed x15 -> x1, local copies, waits for them, and re-layouts: 6.39 us -> 0.97 us
where the time goes in v6:
time: 44.8 us; the launch traced here: 44.6 us
  Pallas kernels  43.6 us (97%)
  local copies, waits for them, and re-layouts  0.97 us (2%)
    pallas_call x1, Pallas kernels, body(): pl.pallas_call(trunk, out_shape=pltpu.VMEM((PC, BAND, BINW), f32), in_spe...  43.6 us
    unnamed x1, local copies, waits for them, and re-layouts  0.97 us

profile of v6, /device:TPU:1, one launch (start us, length us, event | category | flops | bytes accessed | tf_op | source)
XLA Modules:
  0.0 44.6 jit_solution(15329245900586596294)
XLA Ops:
  0.0 43.6 %trunk.1 = f32[32,32,256]{2,1,0:T(8,128)S(1)} custom-call(s32[4]{0:T(128)} %dil_ref.1, bf16[64,128]{1,0:T(8,128)(2,1)} %feat_in.1, s32[1,64]{1,0:T(1,128)} %bitcast.5, bf16[64,128]{1,0:T(8,128)(2,1)} %bitcast.3, f32[32,32]{1,0:T(8,128)} %emb_in.1, f32[8,9,32,32]{3,2,1,0:T(8,128)} %cw_in.1, f32[8,1,32]{2,1,0:T(1,128)} %bitcast.4), custom_call_target="tpu_custom_call" | custom-call | tf_op jit(solution)/shard_map/trunk/pallas_call | solution.py:357
  43.7 1.0 %copy.9 = f32[32,32,256]{2,1,0:T(8,128)} copy(f32[32,32,256]{2,1,0:T(8,128)S(1)} %trunk.1) | data formatting | bytes 2097152

commit v7 on v6

--- a/solution.py
+++ b/solution.py
@@ -65,14 +65,10 @@
 
 def trunk(dil_ref, feat_in, del_in, proj_in, emb_in, cw_in, cb_in, out_ref,
           feat_ref, del_ref, proj_ref, emb_ref, cw_ref, cb_ref, in_sem,
-          kept, land, emb_land, w_ref, bias_ref, row_s, col_s, v_ref, ya, yb, m_ref, v2_ref, ya2, yb2, o_ref, halo1, halo2,
-          send, recv, esend, erecv, msend, mrecv, hsend, hrecv, osem):
+          kept, land, emb_land, emb_s, w_ref, bias_ref, row_s, col_s, v_ref, ya, yb, m_ref, v2_ref, ya2, yb2, halo1, halo2,
+          send, recv, esend, erecv, msend, mrecv, hsend, hrecv):
     row = lax.axis_index("rows")
     band = lax.axis_index("band")
-    arguments = ((feat_in, feat_ref), (del_in, del_ref), (emb_in, emb_ref), (proj_in, proj_ref), (cb_in, cb_ref), (cw_in, cw_ref))
-    fetch = [pltpu.make_async_copy(src, dst, in_sem.at[i]) for i, (src, dst) in enumerate(arguments)]
-    for copy in fetch:
-        copy.start()
     near = [(row, lax.rem(band + d, 4)) for d in range(1, 4)]
     upper = lax.div(band, 2)
     far_row = jnp.clip(row + 2 * upper - 1, 0, ROWS - 1)
@@ -95,6 +91,10 @@
         greet(row + 1, 0)
         greet(row + 1, 1)
 
+    arguments = ((feat_in, feat_ref), (del_in, del_ref), (emb_in, emb_ref), (proj_in, proj_ref), (cb_in, cb_ref), (cw_in, cw_ref))
+    fetch = [pltpu.make_async_copy(src, dst, in_sem.at[i]) for i, (src, dst) in enumerate(arguments)]
+    for copy in fetch:
+        copy.start()
     fetch[0].wait()
     fetch[1].wait()
     same = lax.broadcasted_iota(jnp.int32, (64, 64), 0) == lax.broadcasted_iota(jnp.int32, (64, 64), 1)
@@ -165,25 +165,40 @@
     def arrived(buf, sem):
         pltpu.make_async_copy(buf, buf, sem).wait()
 
-    for d in range(1, 4):
-        b = lax.rem(band + d, 4)
-        arrived(slot(2 + b), recv.at[2 + b])
-        arrived(emb_land.at[b], erecv.at[b])
-
-    @pl.when(row > 0)
-    def _():
-        for i in (0, 1):
-            arrived(slot(i), recv.at[i])
-
-    @pl.when(row < ROWS - 1)
-    def _():
-        for i in (6, 7):
-            arrived(slot(i), recv.at[i])
-
     half = lax.rem(band, 2)
     pair = lax.div(band, 2)
     other = band + 1 - 2 * half
     u0 = 64 * half - HALO
+    first_q = HALO - HALO * half
+    for d in range(1, 4):
+        b = lax.rem(band + d, 4)
+        arrived(emb_land.at[b], erecv.at[b])
+
+    lanes = lax.broadcasted_iota(jnp.int32, (PC, BAND), 1)
+
+    def spread(t, carry):
+        for s in range(24):
+            q = first_q + t * 24 + s
+            u = u0 + q
+            emb = jnp.where(lanes == (u & 31), emb_land[u >> 5], 0.0)
+            emb_s[q] = jnp.broadcast_to(jnp.sum(emb, axis=1, keepdims=True), (PC, 128))
+        return carry
+
+    lax.fori_loop(0, 3, spread, 0)
+    for d in range(1, 4):
+        b = lax.rem(band + d, 4)
+        arrived(slot(2 + b), recv.at[2 + b])
+
+    @pl.when(row > 0)
+    def _():
+        for i in (0, 1):
+            arrived(slot(i), recv.at[i])
+
+    @pl.when(row < ROWS - 1)
+    def _():
+        for i in (6, 7):
+            arrived(slot(i), recv.at[i])
+
     skip = 128 - 128 * pair
     bin0 = row * BINW - 160 + 64 * pair
     projected = lax.dot_general(
@@ -192,15 +207,14 @@
     row_s[...] = pltpu.roll(projected[:PC], 32 + (W1 - 64) * pair, 1)
     col_s[...] = projected[PC:]
     bins = lax.broadcasted_iota(jnp.int32, (1, W1), 1) + bin0
-    lanes = lax.broadcasted_iota(jnp.int32, (PC, BAND), 1)
 
     def start_rows(t, carry):
         for s in range(24):
-            q = HALO - HALO * half + t * 24 + s
+            q = first_q + t * 24 + s
             u = u0 + q
             col = pltpu.roll(col_s[...], lax.rem(2 * W1 + 96 - 64 * pair - u, W1), 1)
-            emb = jnp.where(lanes == (u & 31), emb_land[u >> 5], 0.0)
-            x = jnp.maximum(row_s[...] + col + jnp.sum(emb, axis=1, keepdims=True), 0.0)
+            emb = jnp.concatenate([emb_s[q]] * (W1 // 128), axis=1)
+            x = jnp.maximum(row_s[...] + col + emb, 0.0)
             x = jnp.where(valid_of(u, bins), x, 0.0)
             v_ref[q] = x
             split_store(ya, q, x)
@@ -252,20 +266,11 @@
     def keep(q, value):
         m_ref[u0 + q] = v_ref[q] + value
 
-    def last_step(t, carry):
+    for t in range(4):
         conv_rows(ctx3, HALO + 16 * t * pair + (48 - 16 * t) * (1 - pair), 16, keep)
-
-        @pl.when(t < 2)
-        def _():
-            swap(t, half, 16).start()
-
-        @pl.when(t == 2)
-        def _():
-            swap(2, half, 12).start()
-
-        return carry
-
-    lax.fori_loop(0, 4, last_step, 0)
+        if t < 3:
+            swap(t, half, 16 if t < 2 else 12).start()
+
     u2 = band * BAND - 32 + 24 * half
     bins2 = lax.broadcasted_iota(jnp.int32, (1, W2), 1) + (bin0 + skip)
 
@@ -321,21 +326,11 @@
     ctx7 = context(7, yb2, u2, bins2)
 
     def emit(q, value):
-        o_ref[q - first] = pltpu.roll(v2_ref[q] + value, shift, 1)[:, :BINW]
-
-    def out_copy(j):
-        return pltpu.make_async_copy(o_ref.at[j], out_ref.at[:, j, :], osem.at[j])
-
-    def finish(low, high, count):
-        rows2(ctx7, low, high, count, emit)
-        for r in range(count):
-            out_copy(low + (high - low) * half - first + r).start()
-
-    finish(32, 16, 24)
+        out_ref[:, q - first, :] = pltpu.roll(v2_ref[q] + value, shift, 1)[:, :BINW]
+
+    rows2(ctx7, 32, 16, 24, emit)
     land2(2, yb2)
-    finish(56, 8, 8)
-    for j in range(BAND):
-        out_copy(j).wait()
+    rows2(ctx7, 56, 8, 8, emit)
     for d, (r, b) in enumerate(near):
         send_to(r, b, 2 + band, d).wait_send()
         send_emb(d, r, b).wait_send()
@@ -347,7 +342,6 @@
 
 
 smem = pl.BlockSpec(memory_space=pltpu.SMEM)
-hbm = pl.BlockSpec(memory_space=pl.ANY)
 f32 = jnp.float32
 bf16 = jnp.bfloat16
 
@@ -358,7 +352,7 @@
         trunk,
         out_shape=pltpu.VMEM((PC, BAND, BINW), f32),
         in_specs=[smem] + [pl.BlockSpec(memory_space=pltpu.HBM)] * 6,
-        out_specs=hbm,
+        out_specs=pl.BlockSpec(memory_space=pltpu.VMEM),
         scratch_shapes=[
             pltpu.VMEM((64, 128), bf16),
             pltpu.VMEM((1, 64), jnp.int32),
@@ -370,6 +364,7 @@
             pltpu.VMEM((64, 128), bf16),
             pltpu.VMEM((FW, 128), bf16),
             pltpu.VMEM((4, PC, BAND), f32),
+            pltpu.VMEM((R1, PC, 128), f32),
             pltpu.VMEM((8, 192, 192), bf16),
             pltpu.VMEM((8, PC, 128), f32),
             pltpu.VMEM((PC, W1), f32),
@@ -381,10 +376,9 @@
             pltpu.VMEM((R2, PC, W2), f32),
             pltpu.VMEM((R2, 2 * PC, W2), bf16),
             pltpu.VMEM((R2, 2 * PC, W2), bf16),
-            pltpu.VMEM((BAND, PC, BINW), f32),
             pltpu.VMEM((3, HALO, 2 * PC, W1), bf16),
             pltpu.VMEM((3, HALO, 2 * PC, W2), bf16),
-            dma((7,)), dma((8,)), dma((3,)), dma((4,)), dma((3,)), dma((3,)), dma((6,)), dma((6,)), dma((BAND,)),
+            dma((7,)), dma((8,)), dma((3,)), dma((4,)), dma((3,)), dma((3,)), dma((6,)), dma((6,)),
         ],
         compiler_params=pltpu.CompilerParams(
             collective_id=0, has_side_effects=True, vmem_limit_bytes=55 * 2 ** 20),

time: 44.8 us -> 43.4 us (0.969)
  Pallas kernels: 43.6 us -> 42.2 us
    pallas_call x1, Pallas kernels: 43.6 us -> 42.2 us  [body(): pl.pallas_call(trunk, out_shape=pltpu.VMEM((PC, BAND, BINW), f32), in_spe...]
where the time goes in v7:
time: 43.4 us; the launch traced here: 43.2 us
  Pallas kernels  42.2 us (97%)
  local copies, waits for them, and re-layouts  0.97 us (2%)
    pallas_call x1, Pallas kernels, body(): pl.pallas_call(trunk, out_shape=pltpu.VMEM((PC, BAND, BINW), f32), in_spe...  42.2 us
    unnamed x1, local copies, waits for them, and re-layouts  0.97 us

profile of v7, /device:TPU:1, one launch (start us, length us, event | category | flops | bytes accessed | tf_op | source)
XLA Modules:
  0.0 43.2 jit_solution(17319630879123084648)
XLA Ops:
  0.0 42.2 %trunk.1 = f32[32,32,256]{2,1,0:T(8,128)S(1)} custom-call(s32[4]{0:T(128)} %dil_ref.1, bf16[64,128]{1,0:T(8,128)(2,1)} %feat_in.1, s32[1,64]{1,0:T(1,128)} %bitcast.5, bf16[64,128]{1,0:T(8,128)(2,1)} %bitcast.3, f32[32,32]{1,0:T(8,128)} %emb_in.1, f32[8,9,32,32]{3,2,1,0:T(8,128)} %cw_in.1, f32[8,1,32]{2,1,0:T(1,128)} %bitcast.4), custom_call_target="tpu_custom_call" | custom-call | tf_op jit(solution)/shard_map/trunk/pallas_call | solution.py:351
  42.2 1.0 %copy.9 = f32[32,32,256]{2,1,0:T(8,128)} copy(f32[32,32,256]{2,1,0:T(8,128)S(1)} %trunk.1) | data formatting | bytes 2097152

commit v8 on v7

--- a/solution.py
+++ b/solution.py
@@ -120,6 +120,9 @@
             emb_ref, emb_land.at[band], esend.at[d], erecv.at[band],
             device_id={"rows": r, "band": b}, device_id_type=MESH)
 
+    for d, (r, b) in enumerate(near):
+        send_emb(d, r, b).start()
+
     @pl.when(far)
     def _():
         for d in range(4):
@@ -127,8 +130,6 @@
 
     for d, (r, b) in enumerate(near):
         send_to(r, b, 2 + band, d).start()
-    for d, (r, b) in enumerate(near):
-        send_emb(d, r, b).start()
     land[pl.ds(128 + 64 * band, 64), :] = kept[...]
     emb_land[band] = emb_ref[...]
     none = jnp.zeros((128, 128), jnp.bfloat16)
@@ -177,14 +178,14 @@
     lanes = lax.broadcasted_iota(jnp.int32, (PC, BAND), 1)
 
     def spread(t, carry):
-        for s in range(24):
-            q = first_q + t * 24 + s
+        for s in range(36):
+            q = first_q + t * 36 + s
             u = u0 + q
             emb = jnp.where(lanes == (u & 31), emb_land[u >> 5], 0.0)
             emb_s[q] = jnp.broadcast_to(jnp.sum(emb, axis=1, keepdims=True), (PC, 128))
         return carry
 
-    lax.fori_loop(0, 3, spread, 0)
+    lax.fori_loop(0, 2, spread, 0)
     for d in range(1, 4):
         b = lax.rem(band + d, 4)
         arrived(slot(2 + b), recv.at[2 + b])
@@ -209,8 +210,8 @@
     bins = lax.broadcasted_iota(jnp.int32, (1, W1), 1) + bin0
 
     def start_rows(t, carry):
-        for s in range(24):
-            q = first_q + t * 24 + s
+        for s in range(36):
+            q = first_q + t * 36 + s
             u = u0 + q
             col = pltpu.roll(col_s[...], lax.rem(2 * W1 + 96 - 64 * pair - u, W1), 1)
             emb = jnp.concatenate([emb_s[q]] * (W1 // 128), axis=1)
@@ -220,7 +221,7 @@
             split_store(ya, q, x)
         return carry
 
-    lax.fori_loop(0, 3, start_rows, 0)
+    lax.fori_loop(0, 2, start_rows, 0)
 
     def context(n, src, u0, bins):
         bias = jnp.concatenate([bias_ref[n]] * (bins.shape[1] // 128), axis=1)

time: 43.4 us -> 42.7 us (0.984)
  Pallas kernels: 42.2 us -> 41.6 us
    pallas_call x1, Pallas kernels: 42.2 us -> 41.6 us  [body(): pl.pallas_call(trunk, out_shape=pltpu.VMEM((PC, BAND, BINW), f32), in_spe...]
where the time goes in v8:
time: 42.7 us; the launch traced here: 42.6 us
  Pallas kernels  41.6 us (97%)
  local copies, waits for them, and re-layouts  0.97 us (2%)
    pallas_call x1, Pallas kernels, body(): pl.pallas_call(trunk, out_shape=pltpu.VMEM((PC, BAND, BINW), f32), in_spe...  41.6 us
    unnamed x1, local copies, waits for them, and re-layouts  0.97 us

profile of v8, /device:TPU:1, one launch (start us, length us, event | category | flops | bytes accessed | tf_op | source)
XLA Modules:
  0.0 42.6 jit_solution(3660619830837200295)
XLA Ops:
  0.0 41.6 %trunk.1 = f32[32,32,256]{2,1,0:T(8,128)S(1)} custom-call(s32[4]{0:T(128)} %dil_ref.1, bf16[64,128]{1,0:T(8,128)(2,1)} %feat_in.1, s32[1,64]{1,0:T(1,128)} %bitcast.5, bf16[64,128]{1,0:T(8,128)(2,1)} %bitcast.3, f32[32,32]{1,0:T(8,128)} %emb_in.1, f32[8,9,32,32]{3,2,1,0:T(8,128)} %cw_in.1, f32[8,1,32]{2,1,0:T(1,128)} %bitcast.4), custom_call_target="tpu_custom_call" | custom-call | tf_op jit(solution)/shard_map/trunk/pallas_call | solution.py:352
  41.6 1.0 %copy.9 = f32[32,32,256]{2,1,0:T(8,128)} copy(f32[32,32,256]{2,1,0:T(8,128)S(1)} %trunk.1) | data formatting | bytes 2097152
